TPU v7x, 32 devices: a whole 2x2x4 slice. The times are simulated.
32 devices in a mesh: depth: 1, eta: 32 (over z, y, x, core).
Axes of the slice: x: 2, y: 2, z: 4, core: 2. Of those that a mesh axis runs over, the one named last changes fastest.
Arguments:
- field_in: bfloat16 [2, 128, 32, 2048], P('depth', 'eta'), may hold values from -6 to 6
- grad_out: bfloat16 [2, 128, 32, 2048], P('depth', 'eta'), may hold values from -6 to 6
- spectral_weight: bfloat16 [2, 64, 64, 1024], P(None, 'eta'), may hold values from -0.75 to 0.75
- mlp_in: bfloat16 [32, 64], replicated, may hold values from -1 to 1
- mlp_bias: float32 [64], replicated, may hold values from -3 to 3
- mlp_out: bfloat16 [64, 32], replicated, may hold values from -0.75 to 0.75
Outputs:
- grad_in: float32 [2, 128, 32, 2048], P('depth', 'eta')
- grad_spectral: float32 [2, 64, 64, 1024], P(None, 'eta', 'depth')
- grad_mlp_in: float32 [32, 64], replicated
- grad_mlp_out: float32 [64, 32], replicated
- grad_mlp_bias: float32 [64], replicated
All inputs are finite; a program needn't handle non-finite values.
Results may differ from a plain program's by a relative error of at most 0.0087.
Values may be sent and summed in bfloat16 or wider, within the bound.
No kernel may reach another device: no remote copies, remote signals or barrier semaphores. Data moves between devices by JAX's collectives and lax.ppermute only.
A program may use at most 128 MiB of HBM per device.

v0:
```python
import math

import jax
import jax.numpy as jnp
from jax import lax
from jax.sharding import PartitionSpec as P


def phi_tables(n_phi, n_modes):
    cells = jnp.arange(n_phi, dtype=jnp.int32)
    index = jnp.arange(n_modes, dtype=jnp.int32)
    freq = jnp.where(index < n_modes // 2, index, n_phi - n_modes + index)
    theta = 2.0 * math.pi / n_phi * (cells[:, None] * freq[None, :] % n_phi).astype(jnp.float32)
    pairs = jnp.stack([jnp.cos(theta), -jnp.sin(theta)], axis=-1).reshape(n_phi, 2 * n_modes)
    forward = (pairs / math.sqrt(n_phi)).astype(jnp.bfloat16)
    inverse = (pairs.T / math.sqrt(n_modes)).astype(jnp.bfloat16)
    return (forward, inverse)


def eta_tables(n_eta, n_modes, start, count):
    cells = start + jnp.arange(count, dtype=jnp.int32)
    index = jnp.arange(n_modes, dtype=jnp.int32)
    phase = 2.0 * math.pi / n_eta * (cells[:, None] * index[None, :] % n_eta).astype(jnp.float32)
    cosine = jnp.cos(phase)
    sine = jnp.sin(phase)
    return (
        (cosine / math.sqrt(n_eta)).astype(jnp.bfloat16),
        (sine / math.sqrt(n_eta)).astype(jnp.bfloat16),
        cosine.T / math.sqrt(n_modes),
        sine.T / math.sqrt(n_modes),
    )


def gelu_slope(value):
    normal_cdf = 0.5 * (1.0 + lax.erf(value / math.sqrt(2.0)))
    return normal_cdf + value * jnp.exp(-0.5 * value * value) / math.sqrt(2.0 * math.pi)


def eta_forward(spectra, eta_cos, eta_sin):
    layers, cells, chans, twice = spectra.shape
    parts = spectra.reshape(layers, cells, chans, twice // 2, 2)
    real_part = parts[..., 0]
    imag_part = parts[..., 1]
    f32 = jnp.float32
    zr = jnp.einsum("decj,em->jdmc", real_part, eta_cos, preferred_element_type=f32) + jnp.einsum(
        "decj,em->jdmc", imag_part, eta_sin, preferred_element_type=f32
    )
    zi = jnp.einsum("decj,em->jdmc", imag_part, eta_cos, preferred_element_type=f32) - jnp.einsum(
        "decj,em->jdmc", real_part, eta_sin, preferred_element_type=f32
    )
    return jnp.stack([zr, zi], axis=2)


def eta_inverse(modes, inv_cos, inv_sin):
    hp = lax.Precision.HIGHEST
    vr = modes[:, :, 0]
    vi = modes[:, :, 1]
    wr = jnp.einsum("jdmc,me->decj", vr, inv_cos, precision=hp) - jnp.einsum(
        "jdmc,me->decj", vi, inv_sin, precision=hp
    )
    wi = jnp.einsum("jdmc,me->decj", vr, inv_sin, precision=hp) + jnp.einsum(
        "jdmc,me->decj", vi, inv_cos, precision=hp
    )
    layers, cells, chans, count = wr.shape
    return (
        jnp.stack([wr, wi], axis=-1).reshape(layers, cells, chans, 2 * count).astype(jnp.bfloat16)
    )


def local(field_in, grad_out, spectral_weight, mlp_in, mlp_bias, mlp_out):
    hp = lax.Precision.HIGHEST
    f32 = jnp.float32
    layers, eta_local, chans, n_phi = field_in.shape
    eta_count = lax.axis_size("eta")
    n_eta = eta_local * eta_count
    owned = spectral_weight.shape[1]
    n_phi_modes = owned * eta_count
    n_eta_modes = spectral_weight.shape[2]
    phi_fwd, phi_inv = phi_tables(n_phi, n_phi_modes)
    weights = spectral_weight.reshape(2, owned, n_eta_modes, chans, chans).astype(f32)
    rr = weights[0]
    ri = weights[1]
    first = lax.axis_index("eta") * eta_local
    eta_cos, eta_sin, inv_cos, inv_sin = eta_tables(n_eta, n_eta_modes, first, eta_local)

    def to_modes(spectra):
        return lax.psum_scatter(
            eta_forward(spectra, eta_cos, eta_sin), "eta", scatter_dimension=0, tiled=True
        )

    def from_modes(modes):
        fields = eta_inverse(lax.all_gather(modes, "eta", axis=0, tiled=True), inv_cos, inv_sin)
        return jnp.dot(fields, phi_inv, preferred_element_type=f32)

    xp = jnp.dot(field_in, phi_fwd, preferred_element_type=f32).astype(jnp.bfloat16)
    zx = to_modes(xp)
    zr = zx[:, :, 0]
    zi = zx[:, :, 1]
    vr = jnp.einsum("kdmc,kmco->kdmo", zr, rr, precision=hp) - jnp.einsum(
        "kdmc,kmco->kdmo", zi, ri, precision=hp
    )
    vi = jnp.einsum("kdmc,kmco->kdmo", zr, ri, precision=hp) + jnp.einsum(
        "kdmc,kmco->kdmo", zi, rr, precision=hp
    )
    spectral = from_modes(jnp.stack([vr, vi], axis=2))
    hidden_pre = (
        jnp.einsum("decp,ch->dehp", field_in, mlp_in, preferred_element_type=f32)
        + mlp_bias[None, None, :, None]
    )
    hidden = jax.nn.gelu(hidden_pre, approximate=False).astype(jnp.bfloat16)
    pre = spectral + jnp.einsum("dehp,hc->decp", hidden, mlp_out, preferred_element_type=f32)
    gpre = (grad_out.astype(f32) * gelu_slope(pre)).astype(jnp.bfloat16)
    gp = jnp.dot(gpre, phi_fwd, preferred_element_type=f32).astype(jnp.bfloat16)
    zg = to_modes(gp)
    gr = zg[:, :, 0]
    gi = zg[:, :, 1]
    local_r = jnp.einsum("kdmc,kdmo->kmco", zr, gr, precision=hp) + jnp.einsum(
        "kdmc,kdmo->kmco", zi, gi, precision=hp
    )
    local_i = jnp.einsum("kdmc,kdmo->kmco", zr, gi, precision=hp) - jnp.einsum(
        "kdmc,kdmo->kmco", zi, gr, precision=hp
    )
    local_grad = jnp.stack([local_r, local_i], axis=0).reshape(2, owned, n_eta_modes, chans * chans)
    factor = math.sqrt(n_phi * n_eta / (n_phi_modes * n_eta_modes))
    grad_spectral = lax.psum_scatter(local_grad, "depth", scatter_dimension=2, tiled=True) * factor
    br = jnp.einsum("kdmo,kmco->kdmc", gr, rr, precision=hp) + jnp.einsum(
        "kdmo,kmco->kdmc", gi, ri, precision=hp
    )
    bi = jnp.einsum("kdmo,kmco->kdmc", gi, rr, precision=hp) - jnp.einsum(
        "kdmo,kmco->kdmc", gr, ri, precision=hp
    )
    back_spec = from_modes(jnp.stack([br, bi], axis=2))
    hidden_grad = jnp.einsum(
        "decp,hc->dehp", gpre, mlp_out, preferred_element_type=f32
    ) * gelu_slope(hidden_pre)
    hidden_gb = hidden_grad.astype(jnp.bfloat16)
    grad_in = (
        grad_out.astype(f32)
        + back_spec
        + jnp.einsum("dehp,ch->decp", hidden_gb, mlp_in, preferred_element_type=f32)
    )
    part_in = jnp.einsum("decp,dehp->ch", field_in, hidden_gb, preferred_element_type=f32)
    part_out = jnp.einsum("dehp,decp->hc", hidden, gpre, preferred_element_type=f32)
    part_bias = jnp.sum(hidden_grad, axis=(0, 1, 3))
    total_in, total_out, total_bias = lax.psum((part_in, part_out, part_bias), ("depth", "eta"))
    norm = 1.0 / math.sqrt(layers * lax.axis_size("depth") * n_eta * n_phi)
    return (grad_in, grad_spectral, total_in * norm, total_out * norm, total_bias * norm)


def solution(mesh):
    return jax.shard_map(
        local,
        mesh=mesh,
        in_specs=(
            P("depth", "eta", None, None),
            P("depth", "eta", None, None),
            P(None, "eta", None, None),
            P(),
            P(),
            P(),
        ),
        out_specs=(P("depth", "eta", None, None), P(None, "eta", "depth", None), P(), P(), P()),
        check_vma=False,
    )
```

profile of v0, /device:TPU:0, one launch (start us, length us, event | category | flops | bytes accessed | tf_op | source)
XLA Modules:
  0.0 579.6 jit_solution(16442367985008307285)
XLA Ops:
  17.4 6.3 %copy.136 = f32[64,2,2,64,32]{3,4,2,1,0:T(8,128)} copy(f32[64,2,2,64,32]{0,3,4,1,2:T(8,128)} %pad_maximum_fusion) | data formatting | bytes 4194304 | tf_op jit(solution)/shard_map/stack | solution.py:51
  30.2 137.3 %reduce-scatter.3.cloned.1.call-done = f32[2,2,2,64,32]{3,4,2,1,0:T(8,128)} async-done(((f32[64,2,2,64,32]{3,4,2,1,0:T(8,128)}), f32[2,2,2,64,32]{3,4,2,1,0:T(8,128)}) %reduce-scatter.3.cloned.1.call-update) | async-done | bytes 65552 | tf_op jit(solution)/shard_map/reduce_scatter | solution.py:87
  176.2 10.8 %fusion.2 = (bf16[2,4,64,2048]{3,2,1,0:T(8,128)(2,1)}, f32[64,2,4,2048]{3,0,2,1:T(8,128)}) fusion(f32[64]{0:T(128)S(1)} %copy-done.15, bf16[2,4,32,2048]{3,2,1,0:T(8,128)(2,1)S(1)} %copy-done, bf16[32,64]{1,0:T(8,128)(2,1)S(1)} %copy-done.13), kind=kOutput, calls=%fused_computation.4 | convolution fusion | flops 136314880 | bytes 7344384 | tf_op jit(solution)/shard_map/decp,ch->dehp/dot_general | solution.py:107
  187.0 60.0 %all-gather.3.cloned.1.call-done = f32[64,2,2,64,32]{4,1,3,0,2:T(2,128)} async-done(((f32[2,2,2,64,32]{4,1,3,0,2:T(2,128)}), f32[64,2,2,64,32]{4,1,3,0,2:T(2,128)}) %all-gather.3.cloned.1.call-update) | async-done | bytes 2097168 | tf_op jit(solution)/shard_map/all_gather | solution.py:92
  247.1 7.8 %slice_bitcast_fusion.2 = (f32[64,2,64,32]{3,1,2,0:T(2,128)}, f32[64,2,64,32]{3,1,2,0:T(2,128)}) fusion(f32[64,2,2,64,32]{4,1,3,0,2:T(2,128)} %all-gather.3.cloned.1.call-done), kind=kLoop, calls=%fused_computation.12 | loop fusion | bytes 4194304 | tf_op jit(solution)/shard_map/squeeze | solution.py:57
  254.8 5.4 copy.145
  260.2 5.0 fusion.104
  265.2 5.0 fusion.111
  270.3 5.9 %copy.146 = f32[64,2,64,32]{2,0,3,1:T(8,128)S(1)} copy(f32[64,2,64,32]{3,1,2,0:T(2,128)} %get-tuple-element.25) | data formatting | bytes 2097152 | tf_op jit(solution)/shard_map/squeeze | solution.py:57
  276.2 5.0 fusion.41
  281.2 5.0 fusion.40
  298.7 6.3 %copy.157 = f32[64,2,2,64,32]{3,4,2,1,0:T(8,128)} copy(f32[64,2,2,64,32]{0,3,4,1,2:T(8,128)} %pad_maximum_fusion.1) | data formatting | bytes 4194304 | tf_op jit(solution)/shard_map/stack | solution.py:51
  305.2 139.2 %reduce-scatter.5.cloned.1.call-done = f32[2,2,2,64,32]{3,4,2,1,0:T(8,128)} async-done(((f32[64,2,2,64,32]{3,4,2,1,0:T(8,128)}), f32[2,2,2,64,32]{3,4,2,1,0:T(8,128)}) %reduce-scatter.5.cloned.1.call-update) | async-done | bytes 65552 | tf_op jit(solution)/shard_map/reduce_scatter | solution.py:87
  457.4 4.2 fusion.208
  463.6 38.8 %all-reduce = (f32[32,64]{1,0:T(8,128)S(1)}, f32[64,32]{0,1:T(8,128)S(1)}, f32[64]{0:T(128)S(1)}) all-reduce(f32[32,64]{1,0:T(8,128)S(1)} %convolution_bitcast_fusion.3, f32[64,32]{0,1:T(8,128)S(1)} %convolution_bitcast_fusion.2, f32[64]{0:T(128)S(1)} %get-tuple-element.43), channel_id=1, replica_groups=mesh['depth'=1,'eta'=32] {'depth','eta'}, use_global_device_ids=true, to_apply=%region_2.3 | all-reduce | flops 4160 | bytes 33280 | tf_op jit(solution)/shard_map/psum | solution.py:145
  507.6 4.4 convolution_subtract_fusion
  517.5 4.6 convolution_add_fusion.1
  529.4 7.8 %slice_bitcast_fusion = (f32[64,2,64,32]{3,1,2,0:T(2,128)}, f32[64,2,64,32]{3,1,2,0:T(2,128)}) fusion(f32[64,2,2,64,32]{4,1,3,0,2:T(2,128)} %all-gather.5.cloned.1.call-done), kind=kLoop, calls=%fused_computation.10 | loop fusion | bytes 4194304 | tf_op jit(solution)/shard_map/squeeze | solution.py:57
  537.2 5.4 copy.164
  542.6 5.0 fusion.101
  547.6 5.0 fusion.108
  552.6 5.7 copy.165
  558.4 5.0 fusion.39
  563.4 5.0 fusion.38
  (109 shorter events, 74.8 us)
Async XLA Ops:
  7.2 3.9 copy-start
  7.2 160.3 %reduce-scatter.3.cloned.1.call-start = ((), (), s32[]{:S(2)}) async-start(), calls=%async_computation.2 | async-start | bytes 4325376 | tf_op jit(solution)/shard_map/reduce_scatter | solution.py:87
  11.1 3.2 copy-start.5
  23.7 1.0 copy-start.12
  23.7 223.3 %all-gather.3.cloned.1.call-start = ((), (), s32[]{:S(2)}) async-start(), calls=%async_computation.3 | async-start | bytes 8650752 | tf_op jit(solution)/shard_map/all_gather | solution.py:92
  26.6 145.8 %copy-start.7 = (bf16[2,64,32,32]{3,2,1,0:T(8,128)(2,1)}, bf16[2,64,32,32]{3,2,1,0:T(8,128)(2,1)S(1)}, u32[]{:S(2)}) copy-start(bf16[2,64,32,32]{3,2,1,0:T(8,128)(2,1)S(1)} %copy.142) | copy-start | bytes 786436
  30.2 146.0 %copy-start.1 = (bf16[2,64,32,32]{3,2,1,0:T(8,128)(2,1)}, bf16[2,64,32,32]{3,2,1,0:T(8,128)(2,1)S(1)}, u32[]{:S(2)}) copy-start(bf16[2,64,32,32]{3,2,1,0:T(8,128)(2,1)S(1)} %copy.139) | copy-start | bytes 786436
  168.5 7.7 %copy-start.11 = (f32[2,2,1,64,32]{4,1,3,0,2:T(2,128)}, f32[2,2,1,64,32]{4,1,3,0,2:T(2,128)S(1)}, u32[]{:S(2)}) copy-start(f32[2,2,1,64,32]{4,1,3,0,2:T(2,128)S(1)} %copy.196) | copy-start | bytes 98308
  168.6 7.5 %copy-start.13 = (bf16[32,64]{1,0:T(8,128)(2,1)S(1)}, bf16[32,64]{1,0:T(8,128)(2,1)}, u32[]{:S(2)}) copy-start(bf16[32,64]{1,0:T(8,128)(2,1)} %param.9) | copy-start | bytes 12292
  168.7 7.5 %copy-start.15 = (f32[64]{0:T(128)S(1)}, f32[64]{0:T(128)}, u32[]{:S(2)}) copy-start(f32[64]{0:T(128)} %param.10) | copy-start | bytes 772
  173.3 271.2 %reduce-scatter.5.cloned.1.call-start = ((), (), s32[]{:S(2)}) async-start(), calls=%async_computation.4 | async-start | bytes 4325376 | tf_op jit(solution)/shard_map/reduce_scatter | solution.py:87
  281.2 6.9 %copy-start.14 = (bf16[64,32]{0,1:T(8,128)(2,1)S(1)}, bf16[64,32]{0,1:T(8,128)(2,1)}, u32[]{:S(2)}) copy-start(bf16[64,32]{0,1:T(8,128)(2,1)} %param.11) | copy-start | bytes 12292
  288.1 4.3 copy-start.6
  291.4 1.0 copy-start.9
  305.0 142.1 %copy-start.2 = (bf16[2,64,32,32]{3,2,1,0:T(8,128)(2,1)S(1)}, bf16[2,64,32,32]{3,2,1,0:T(8,128)(2,1)}, u32[]{:S(2)}) copy-start(bf16[2,64,32,32]{3,2,1,0:T(8,128)(2,1)} %copy-done.1) | copy-start | bytes 786436
  305.0 145.5 %copy-start.8 = (bf16[2,64,32,32]{3,2,1,0:T(8,128)(2,1)S(1)}, bf16[2,64,32,32]{3,2,1,0:T(8,128)(2,1)}, u32[]{:S(2)}) copy-start(bf16[2,64,32,32]{3,2,1,0:T(8,128)(2,1)} %copy-done.7) | copy-start | bytes 786436
  305.0 224.4 %all-gather.5.cloned.1.call-start = ((), (), s32[]{:S(2)}) async-start(), calls=%async_computation.5 | async-start | bytes 8650752 | tf_op jit(solution)/shard_map/all_gather | solution.py:92
  450.5 6.9 %copy-start.10 = (bf16[2,4,32,2048]{3,2,1,0:T(8,128)(2,1)S(1)}, bf16[2,4,32,2048]{3,2,1,0:T(8,128)(2,1)}, u32[]{:S(2)}) copy-start(bf16[2,4,32,2048]{3,2,1,0:T(8,128)(2,1)} %copy-done.9) | copy-start | bytes 3145732
  461.6 1.3 copy-start.3
  568.4 2.3 copy-start.4
Sparse Core Ops, SparseCore 0:
  23.8 143.6 reduce-scatter.2
  173.4 73.6 all-gather.2
  305.1 139.2 reduce-scatter.4
  455.0 74.3 all-gather.4
where the time goes:
time: 586 us; the launch traced here: 580 us
  waiting for transfers between devices  338 us (58%)
  matrix products  99.3 us (17%)
  local copies, waits for them, and re-layouts  74.2 us (13%)
  blocking collectives  38.8 us (7%)
  between operations  14.8 us (3%)
  other arithmetic  13.4 us (2%)
    reduce_scatter x2, waiting for transfers between devices, to_modes(): lax.psum_scatter(eta_forward(spectra, eta_cos, eta_sin), 'eta', scatter_d...  277 us
    all_gather x2, waiting for transfers between devices, from_modes(): lax.all_gather(modes, 'eta', axis=0, tiled=True)  61.8 us
    psum x1, blocking collectives, local(): lax.psum((part_in, part_out, part_bias), ('depth', 'eta'))  38.8 us
    squeeze x4, local copies, waits for them, and re-layouts, eta_inverse(): vi = modes[:, :, 1]  27.2 us
    another operation x2, local copies, waits for them, and re-layouts, eta_forward(): return jnp.stack([zr, zi], axis=2)  12.6 us
  transfers between devices with their start and end apart: 4, of which 4 were waited for; matrix products, arithmetic and copies ran while one was open for 9% of the time, Pallas kernels for 0%

commit v1 on v0

v1 whole, which is shorter than its diff:
```python
import functools
import math

import jax
import jax.numpy as jnp
import numpy as np
from jax import lax
from jax.experimental import pallas as pl
from jax.experimental.pallas import tpu as pltpu
from jax.sharding import PartitionSpec as P

F32 = jnp.float32
BF16 = jnp.bfloat16
LANES = 128
CHUNK = 256
STEP = 512
LIMIT = 32 * 1024 * 1024


def phi_pairs(n_phi, owned, owners):
    n_modes = owned * owners
    index = np.arange(n_modes)
    freq = np.where(index < n_modes // 2, index, n_phi - n_modes + index)
    theta = 2.0 * np.pi / n_phi * ((np.arange(n_phi)[None, :] * freq[:, None]) % n_phi)
    theta = theta.reshape(owners, owned, n_phi).transpose(1, 0, 2)
    return np.stack([np.cos(theta), -np.sin(theta)]).reshape(2 * n_modes, n_phi)


def eta_tables(cells, owners, n_modes):
    n_eta = cells * owners
    phase = 2.0 * np.pi / n_eta * ((np.arange(n_eta)[None, :] * np.arange(n_modes)[:, None]) % n_eta)
    phase = phase.reshape(n_modes, owners, cells).transpose(0, 2, 1).reshape(n_modes, n_eta)
    cos, sin = np.cos(phase), np.sin(phase)
    forward = np.concatenate([cos, sin]) / math.sqrt(n_eta)
    inverse = np.block([[cos.T, -sin.T], [sin.T, cos.T]]) / math.sqrt(n_modes)
    return forward, inverse


def dot(a, b):
    return jnp.dot(a, b, preferred_element_type=F32)


def dot_rows(a, b):
    return lax.dot_general(a, b, (((1,), (1,)), ((), ())), preferred_element_type=F32)


def split(x):
    high = x.astype(BF16)
    return high, (x - high.astype(F32)).astype(BF16)


def gelu_parts(v):
    square = v * v
    capped = jnp.minimum(square, 27.04)
    poly = -6.666758338545128e-08
    for a in (
        3.1052332348022884e-06, -5.041388393796624e-05, -4.473045135442513e-05,
        0.03634451762350441, 0.7978822527967008,
    ):
        poly = poly * capped + a
    half = 0.5 * jnp.tanh(v * poly)
    density = (1.0 / math.sqrt(2.0 * math.pi)) * jnp.exp2((-0.5 / math.log(2.0)) * square)
    return half, half + v * density


def load(src, dst, sem):
    return pltpu.make_async_copy(src, dst, sem)


def columns(j):
    return pl.ds(pl.multiple_of(j * STEP, STEP), STEP)


def iota(shape, axis):
    return lax.broadcasted_iota(jnp.int32, shape, axis)


def expand_table(chans, width):
    rows, cols = iota((2 * chans, width), 0), iota((2 * chans, width), 1)
    return (rows % chans == cols // chans).astype(F32).astype(BF16)


def spread_table(chans, groups):
    shape = (2 * groups * chans, groups * LANES)
    rows, cols = iota(shape, 0) % (groups * chans), iota(shape, 1)
    same = (rows // chans == cols // LANES) & (rows % chans == cols % chans)
    return same.astype(F32).astype(BF16)


def gather_table(chans, groups):
    shape = (groups * LANES, LANES)
    rows, cols = iota(shape, 0), iota(shape, 1)
    same = (rows // LANES == cols // chans) & (rows % chans == cols % chans)
    return same.astype(F32).astype(BF16)


def collect_table(chans):
    shape = (chans * chans, LANES)
    return (iota(shape, 0) // chans == iota(shape, 1)).astype(F32).astype(BF16)


def pack_spectra(spectra, rows_ref, rows, layers, cells, owners, owned):
    width = spectra.shape[1] // (layers * cells)
    for cell in range(cells):
        for part in range(2):
            pieces = []
            for mode in range(owned):
                top = (part * owned + mode) * owners
                for layer in range(layers):
                    left = (layer * cells + cell) * width
                    pieces.append(spectra[top : top + owners, left : left + width])
            rows_ref[pl.ds(cell * 2 + part, owners, rows), :] = jnp.concatenate(pieces, axis=1)


def xp_kernel(field_h, fwd_h, out, field, fwd, rows_ref, sems, *, sizes):
    layers, cells, owners, owned = sizes
    copies = [load(fwd_h, fwd, sems.at[0]), load(field_h, field, sems.at[1])]
    for copy in copies:
        copy.start()
    for copy in copies:
        copy.wait()
    spectra = dot_rows(fwd[...], field[...])
    pack_spectra(spectra, rows_ref, 8, layers, cells, owners, owned)
    out[...] = rows_ref[...].reshape(out.shape).astype(BF16)


def by_cell(weights, cells):
    rows, cols = weights.shape
    wide = jnp.concatenate([jnp.concatenate([weights] * cells, axis=1)] * cells, axis=0)
    same = iota(wide.shape, 0) // rows == iota(wide.shape, 1) // cols
    return jnp.where(same, wide, 0.0).astype(BF16)


def hidden_kernel(field_h, w_in_h, bias_h, w_out_h, _, *refs, first, count, carried):
    sources, (hidden_h, slope_h, base_h), refs = refs[:carried], refs[carried : carried + 3], refs[carried + 3 :]
    targets, refs = refs[:carried], refs[carried:]
    field, w_in, bias, w_out, wide_bias, pre, hidden, slope, base, ins, outs = refs
    carries = [load(a, b, ins.at[2, n]) for n, (a, b) in enumerate(zip(sources, targets))]
    steps = field.shape[1] // STEP
    chans, hid = w_in.shape
    smalls = ((w_in_h, w_in), (bias_h, bias), (w_out_h, w_out))
    small = [load(a, b, ins.at[1, n]) for n, (a, b) in enumerate(smalls)]
    for copy in small:
        copy.start()
    rows = pl.ds(first * chans, count * chans)
    span = lambda j: pl.ds(j * STEP, STEP)
    read = lambda j: load(field_h.at[rows, span(j)], field.at[:, span(j)], ins.at[0, j])
    pairs = ((hidden, hidden_h), (slope, slope_h), (base, base_h))
    write = lambda n, j: load(
        pairs[n][0].at[:, span(j)], pairs[n][1].at[:, span(j)], outs.at[n, j]
    )
    for j in range(steps):
        read(j).start()
    for copy in carries:
        copy.start()
    for copy in small:
        copy.wait()
    wide = by_cell(w_in[...].astype(F32).T, count)
    back = by_cell(w_out[...].astype(F32), count)
    wide_bias[...] = jnp.broadcast_to(bias[...].T, wide_bias.shape)

    def project(j):
        base[:, span(j)] = dot(back, hidden[:, span(j)])
        write(2, j).start()

    for j in range(steps):
        read(j).wait()
        pre[:, span(j)] = dot(wide, field[:, span(j)])
        if j:
            project(j - 1)
        for left in range(j * STEP, (j + 1) * STEP, CHUNK):
            at = slice(left, left + CHUNK)
            for i in range(count):
                tall = slice(i * hid, (i + 1) * hid)
                v = pre[tall, at] + wide_bias[...]
                half, centred = gelu_parts(v)
                hidden[tall, at] = (v * (0.5 + half)).astype(BF16)
                slope[tall, at] = centred.astype(BF16)
        for n in range(2):
            write(n, j).start()
    project(steps - 1)
    for j in range(steps):
        for n in range(3):
            write(n, j).wait()
    for copy in carries:
        copy.wait()


def unpack(blocks, rows_ref, cells, owners):
    rows = blocks.shape[1]
    rows_ref[...] = blocks[...].astype(F32).reshape(rows_ref.shape)
    part = lambda p: jnp.concatenate(
        [rows_ref[pl.ds(cell * 2 + p, owners, rows), :] for cell in range(cells)], axis=0
    )
    return jnp.concatenate([part(0), part(1)], axis=1).astype(BF16)


def modes_of(spectra, forward):
    both = dot(forward[...], spectra)
    half = both.shape[0] // 2
    real = both[:half, :LANES] + both[half:, LANES:]
    imag = both[:half, LANES:] - both[half:, :LANES]
    return jnp.concatenate([real, imag], axis=0)


def fields_of(modes, inverse, rows_ref, rows, cells, owners):
    high, low = split(modes)
    fields = dot(inverse[...], jnp.concatenate([high, low, high], axis=0))
    for part in range(2):
        for cell in range(cells):
            top = (part * cells + cell) * owners
            rows_ref[pl.ds(cell * 2 + part, owners, rows), :] = fields[top : top + owners]


def widen(modes, pick, chans):
    high, low = split(modes[:, pick * chans : (pick + 1) * chans])
    return jnp.concatenate([high, low], axis=1)


def mix_kernel(
    blocks, weights, forward, inverse, out, modes_h, modes, rows_ref, sems, *, sizes,
):
    layers, cells, owners, owned = sizes
    chans = LANES // (layers * owned)
    expand = expand_table(chans, chans * chans)
    gather = gather_table(chans, layers * owned)
    spectra = unpack(blocks, rows_ref, cells, owners)
    z = modes_of(spectra, forward)
    modes[...] = z
    save = load(modes, modes_h, sems.at[0])
    save.start()
    half = z.shape[0] // 2
    groups = []
    for mode in range(owned):
        wide = jnp.concatenate(
            [widen(z, mode * layers + layer, chans) for layer in range(layers)], axis=0
        )
        sums = [[None, None] for _ in range(layers)]
        for left in range(0, weights.shape[3], CHUNK):
            wr = weights[0, mode, :, left : left + CHUNK].astype(F32)
            wi = weights[1, mode, :, left : left + CHUNK].astype(F32)
            x = dot(wide, expand[:, left : left + CHUNK])
            for layer in range(layers):
                top = 2 * layer * half
                xr, xi = x[top : top + half], x[top + half : top + 2 * half]
                for part, t in enumerate((xr * wr - xi * wi, xr * wi + xi * wr)):
                    t = t[:, :LANES] + t[:, LANES:]
                    old = sums[layer][part]
                    sums[layer][part] = t if old is None else old + t
        groups += [jnp.concatenate(pair, axis=0) for pair in sums]
    high, low = split(jnp.concatenate(groups, axis=1))
    mixed = dot(high, gather) + dot(low, gather)
    fields_of(mixed, inverse, rows_ref, 8, cells, owners)
    out[...] = rows_ref[...].reshape(out.shape).astype(BF16)
    save.wait()


def phi_rows(blocks, rows_ref, layers, cells, owners, owned):
    rows = blocks.shape[1]
    rows_ref[...] = blocks[...].astype(F32).reshape(rows_ref.shape)
    chans = LANES // (layers * owned)
    tall = []
    for part in range(2):
        line = [rows_ref[pl.ds(cell * 2 + part, owners, rows), :] for cell in range(cells)]
        for mode in range(owned):
            pieces = []
            for layer in range(layers):
                left = (mode * layers + layer) * chans
                pieces += [line[cell][:, left : left + chans] for cell in range(cells)]
            tall.append(jnp.concatenate(pieces, axis=1))
    return jnp.concatenate(tall, axis=0).T.astype(BF16)


def gpre_kernel(
    blocks, field_h, cot_h, hidden_a, hidden_b, slope_a, slope_b, base_a, base_b,
    fwd_h, inv_h, w_out_h, out, grad_h,
    field, cot, hidden, slope, base, fwd, inv, w_out, gpre, grad_b, waves, back, pre, grad,
    rows_in, rows_out, slab, ins, outs, *, sizes,
):
    layers, cells, owners, owned = sizes
    n_phi = field.shape[1]
    chans, hid = w_out.shape
    thin, tall = base_a.shape[0], hidden_a.shape[0]
    count = thin // chans
    rows = lambda n: pl.ds(n * thin, thin)
    high = lambda n: pl.ds(n * tall, tall)
    whole = [load(a, b, ins.at[0, n]) for n, (a, b) in enumerate(((w_out_h, w_out), (inv_h, inv), (fwd_h, fwd)))]
    early = [
        [
            load((base_a, base_b)[n], base.at[rows(n), :], ins.at[1 + n, 0]),
            load(cot_h.at[rows(n), :], cot.at[rows(n), :], ins.at[1 + n, 1]),
            load((slope_a, slope_b)[n], slope.at[high(n), :], ins.at[1 + n, 2]),
        ]
        for n in range(2)
    ]
    late = [
        [
            load((hidden_a, hidden_b)[n], hidden.at[high(n), :], ins.at[1 + n, 3]),
            load(field_h.at[rows(n), :], field.at[rows(n), :], ins.at[1 + n, 4]),
        ]
        for n in range(2)
    ]
    writes = [load(grad_b.at[high(n), :], grad_h.at[high(n), :], outs.at[n]) for n in range(2)]
    for copy in (*whole[:2], *early[0], *early[1], whole[2], *late[0], *late[1]):
        copy.start()
    waves[...] = phi_rows(blocks, rows_in, layers, cells, owners, owned)
    whole[0].wait()
    back[...] = by_cell(w_out[...].astype(F32).T, count)
    whole[1].wait()

    def products(n):
        here, up = slice(n * thin, (n + 1) * thin), slice(n * tall, (n + 1) * tall)
        spectra = dot_rows(fwd[...], gpre[here, :])
        part_out = dot_rows(hidden[up, :], gpre[here, :])
        part_in = dot_rows(grad_b[up, :], field[here, :])
        diagonal = lambda x: sum(
            x[i * hid : (i + 1) * hid, i * chans : (i + 1) * chans] for i in range(count)
        )
        return spectra, diagonal(part_in), diagonal(part_out)

    total = jnp.zeros((hid, LANES), F32)
    results = []
    for n in range(2):
        here, up = slice(n * thin, (n + 1) * thin), slice(n * tall, (n + 1) * tall)
        pre[here, :] = dot(waves[here, :], inv[...])
        for copy in early[n]:
            copy.wait()
        if n:
            for copy in (whole[2], *late[0]):
                copy.wait()
            results.append(products(0))
        for left in range(0, n_phi, CHUNK):
            at = slice(left, left + CHUNK)
            for top in range(here.start, here.stop, hid):
                tile = slice(top, top + hid)
                g = 0.5 + gelu_parts(pre[tile, at] + base[tile, at])[1]
                gpre[tile, at] = (cot[tile, at].astype(F32) * g).astype(BF16)
        for left in range(0, n_phi, STEP):
            grad[up, left : left + STEP] = dot(back[...], gpre[here, left : left + STEP])
        for left in range(0, n_phi, CHUNK):
            at = slice(left, left + CHUNK)
            for top in range(up.start, up.stop, hid):
                tile = slice(top, top + hid)
                g = grad[tile, at] * (0.5 + slope[tile, at].astype(F32))
                grad_b[tile, at] = g.astype(BF16)
                total = total + (g[:, :LANES] + g[:, LANES:])
        writes[n].start()
    for copy in late[1]:
        copy.wait()
    results.append(products(1))
    spectra = jnp.concatenate([r[0] for r in results], axis=1)
    pack_spectra(spectra, rows_out, 16, layers, cells, owners, owned)
    part_in, part_out = results[0][1] + results[1][1], results[0][2] + results[1][2]
    bias = jnp.sum(total, axis=1, keepdims=True)
    zeros = jnp.zeros((hid, LANES - 2 * chans), F32)
    full = jnp.concatenate([part_in, part_out, zeros], axis=1)
    full = jnp.where(iota((hid, LANES), 1) == 2 * chans, bias, full)
    high = full.astype(BF16).astype(F32)
    each = hid // owners
    for at, value in enumerate((high, full - high)):
        slab[...] = value
        for row in range(each):
            rows_out[pl.ds(8 + at * each + row, owners, 16), :] = slab[pl.ds(row, owners, each), :]
    for row in range(8 + 2 * each, 16):
        rows_out[pl.ds(row, owners, 16), :] = jnp.zeros((owners, LANES), F32)
    out[...] = rows_out[...].reshape(out.shape).astype(BF16)
    for write in writes:
        write.wait()


def mlp_grad_kernel(cot_h, grad_h, w_in_h, inv_h, out, inv, cot, grad_b, w_in, sems, *, count):
    chans, hid = w_in.shape
    half = cot.shape[0] // 2
    copies = [load(w_in_h, w_in, sems.at[0])]
    for n in range(2):
        low, high = pl.ds(n * half, half), pl.ds(n * half // chans * hid, half // chans * hid)
        copies.append(load(cot_h.at[low, :], cot.at[low, :], sems.at[1 + 2 * n]))
        copies.append(load(grad_h.at[high, :], grad_b.at[high, :], sems.at[2 + 2 * n]))
    copies.append(load(inv_h, inv, sems.at[5]))
    for copy in copies:
        copy.start()
    copies[0].wait()
    weights = by_cell(w_in[...].astype(F32), count)
    for n in range(2):
        for copy in copies[1 + 2 * n : 3 + 2 * n]:
            copy.wait()
        low = slice(n * half, (n + 1) * half)
        high = slice(low.start // chans * hid, low.stop // chans * hid)
        for left in range(0, cot.shape[1], STEP):
            at = slice(left, left + STEP)
            out[low, at] = cot[low, at].astype(F32) + dot(weights, grad_b[high, at])
    copies[5].wait()


def back_kernel(
    blocks, weights, forward, inverse, _, out, modes_h, modes, rows_ref, sems, *, sizes, each,
):
    layers, cells, owners, owned = sizes
    chans = LANES // (layers * owned)
    spread = spread_table(chans, layers * owned)
    collect = collect_table(chans)
    spectra = unpack(blocks, rows_ref, cells, owners)
    z = modes_of(spectra, forward)
    modes[...] = z
    save = load(modes, modes_h, sems.at[0])
    save.start()
    totals = []
    for row in range(each):
        at = 8 + row
        total = jnp.sum(
            rows_ref[pl.ds(at, owners, 16), :] + rows_ref[pl.ds(at + each, owners, 16), :],
            axis=0,
            keepdims=True,
        )
        totals.append(total)
    half = z.shape[0] // 2
    high, low = split(z)
    wide = dot(jnp.concatenate([high, low], axis=1), spread)
    pieces = []
    for mode in range(owned):
        acc = None
        for left in range(0, weights.shape[3], CHUNK):
            wr = weights[0, mode, :, left : left + CHUNK].astype(F32)
            wi = weights[1, mode, :, left : left + CHUNK].astype(F32)
            terms = []
            for layer in range(layers):
                pick = (mode * layers + layer) * LANES
                g = jnp.concatenate([wide[:, pick : pick + LANES]] * (CHUNK // LANES), axis=1)
                gr, gi = g[:half], g[half:]
                terms += [(gr * wr + gi * wi).astype(BF16), (gi * wr - gr * wi).astype(BF16)]
            s = dot(jnp.concatenate(terms, axis=0), collect[left : left + CHUNK, :])
            acc = s if acc is None else acc + s
        acc = [acc[2 * n * half : 2 * (n + 1) * half] for n in range(layers)]
        pieces += [a[:, :chans] for a in acc]
    fields_of(jnp.concatenate(pieces, axis=1), inverse, rows_ref, 16, cells, owners)
    for row, total in enumerate(totals):
        high = total.astype(BF16).astype(F32)
        rows_ref[pl.ds(8 + row, owners, 16), :] = jnp.broadcast_to(high, (owners, LANES))
        rows_ref[pl.ds(8 + each + row, owners, 16), :] = jnp.broadcast_to(total - high, (owners, LANES))
    out[...] = rows_ref[...].reshape(out.shape).astype(BF16)
    save.wait()


def weight_grad_kernel(zx_h, zg_h, out_h, zx, zg, out, sems, *, sizes, factor):
    layers, owned = sizes[0], sizes[3]
    chans = LANES // (layers * owned)
    copies = [load(a, b, sems.at[n]) for n, (a, b) in enumerate(((zx_h, zx), (zg_h, zg)))]
    for copy in copies:
        copy.start()
    expand = expand_table(chans, chans * chans)
    spread = spread_table(chans, layers * owned)
    for copy in copies:
        copy.wait()
    z = zx[...] * factor
    half = z.shape[0] // 2
    high, low = split(zg[...])
    wide = dot(jnp.concatenate([high, low], axis=1), spread)
    saves = []
    for mode in range(owned):
        split_z = [widen(z, mode * layers + layer, chans) for layer in range(layers)]
        for left in range(0, out.shape[3], CHUNK):
            real = imag = 0.0
            for layer in range(layers):
                x = dot(split_z[layer], expand[:, left : left + CHUNK])
                xr, xi = x[:half], x[half:]
                pick = (mode * layers + layer) * LANES
                g = jnp.concatenate([wide[:, pick : pick + LANES]] * (CHUNK // LANES), axis=1)
                gr, gi = g[:half], g[half:]
                real = real + (xr * gr + xi * gi)
                imag = imag + (xr * gi - xi * gr)
            out[0, mode, :, left : left + CHUNK] = real
            out[1, mode, :, left : left + CHUNK] = imag
        for part in range(2):
            saves.append(
                load(out.at[part, mode], out_h.at[part, mode], sems.at[2 + part * owned + mode])
            )
            saves[-1].start()
    for save in saves:
        save.wait()


def final_kernel(
    blocks, base, inv, _, out_h, in_h, out_w_h, bias_h, out, rows_ref, slab, turned, outs, *, sizes, norm,
):
    layers, cells, owners, owned = sizes
    chans = in_h.shape[0]
    count = 4
    span = base.shape[0] // count
    waves = phi_rows(blocks, rows_ref, layers, cells, owners, owned)
    hid = slab.shape[0]
    each = hid // owners
    for row in range(each):
        slab[pl.ds(row, owners, each), :] = (
            rows_ref[pl.ds(8 + row, owners, 16), :] + rows_ref[pl.ds(8 + each + row, owners, 16), :]
        ) * norm
    turned[...] = slab[...].T
    writes = [
        load(turned.at[pl.ds(n * chans, h.shape[0]), :], h, outs.at[1, n])
        for n, h in enumerate((in_h, out_w_h, bias_h))
    ]
    for write in writes:
        write.start()
    for j in range(count):
        here, rows = slice(j * span, (j + 1) * span), pl.ds(j * span, span)
        for left in range(0, base.shape[1], STEP):
            at = slice(left, left + STEP)
            out[here, at] = base[here, at] + dot(waves[here], inv[:, at])
        writes.append(load(out.at[rows, :], out_h.at[rows, :], outs.at[0, j]))
        writes[-1].start()
    for write in writes:
        write.wait()


def call(kernel, ins, outs, scratch, flops, *args, **static):
    space = {"h": pltpu.HBM, "v": pltpu.VMEM, "w": pltpu.VMEM}
    keep = {"h": pltpu.HBM, "w": pltpu.VMEM}
    shapes = [jax.ShapeDtypeStruct(s, d) for _, s, d in outs]
    size = lambda x: math.prod(x.shape) * x.dtype.itemsize
    moved = sum(size(x) for x in (*args, *shapes))
    args = [
        pltpu.with_memory_space_constraint(x, keep[k]) if k in keep else x
        for k, x in zip(ins, args)
    ]
    return pl.pallas_call(
        functools.partial(kernel, **static),
        out_shape=[
            keep[o[0]](x.shape, x.dtype) if o[0] in keep else x for o, x in zip(outs, shapes)
        ],
        in_specs=[pl.BlockSpec(memory_space=space[k]) for k in ins],
        out_specs=[pl.BlockSpec(memory_space=space[k]) for k, _, _ in outs],
        scratch_shapes=[
            pltpu.SemaphoreType.DMA(s) if d is None else pltpu.VMEM(s, d) for s, d in scratch
        ],
        compiler_params=pltpu.CompilerParams(vmem_limit_bytes=LIMIT),
        cost_estimate=pl.CostEstimate(
            flops=flops,
            bytes_accessed=moved,
            transcendentals=0,
        ),
    )(*args)


def local(field_in, grad_out, spectral_weight, mlp_in, mlp_bias, mlp_out):
    layers, cells, chans, n_phi = field_in.shape
    owners = lax.axis_size("eta")
    depth = lax.axis_size("depth")
    n_eta = cells * owners
    owned = spectral_weight.shape[1]
    n_eta_modes = spectral_weight.shape[2]
    n_phi_modes = owned * owners
    hid = mlp_in.shape[1]
    count = layers * cells
    each = hid // owners
    sizes = (layers, cells, owners, owned)
    pairs = phi_pairs(n_phi, owned, owners)
    phi_fwd = jnp.asarray(pairs / math.sqrt(n_phi), BF16)
    phi_inv = jnp.asarray(pairs / math.sqrt(n_phi_modes), BF16)
    forward, inverse = eta_tables(cells, owners, n_eta_modes)
    forward = jnp.asarray(forward, BF16)
    inverse_high = inverse.astype(BF16)
    inverse_low = (inverse - inverse_high.astype(np.float64)).astype(BF16)
    inverse = jnp.asarray(np.concatenate([inverse_high, inverse_high, inverse_low], axis=1))

    thin = (count * chans, n_phi)
    tall = (count * hid, n_phi)
    field = field_in.reshape(thin)
    cot = grad_out.reshape(thin)
    w_out = mlp_out.T
    steps = n_phi // STEP
    exchange = lambda x: lax.all_to_all(x, "eta", 0, 0, tiled=True)
    small = (owners, 8, LANES)
    large = (owners, 16, LANES)
    modes = (2 * n_eta_modes, LANES)
    small_rows = ((owners * 8, LANES), F32)
    large_rows = ((owners * 16, LANES), F32)
    table = ((2 * n_phi_modes, n_phi), BF16)
    grid_mul = 2 * count * n_phi * chans

    (xp,) = call(
        xp_kernel, "hh", [("w", small, BF16)],
        [(thin, BF16), table, small_rows, ((2,), None)],
        grid_mul * 2 * n_phi_modes, field, phi_fwd, sizes=sizes,
    )
    xp = exchange(xp)
    half = count // 2
    part = (half * hid, n_phi)
    half_thin = (half * chans, n_phi)

    def hidden_half(first, after, *carried):
        return call(
            hidden_kernel, "hhhhh" + "h" * len(carried),
            [
                ("h", part, BF16), ("h", part, BF16), ("h", half_thin, F32),
                *(("w", x.shape, x.dtype) for x in carried),
            ],
            [
                (half_thin, BF16), (mlp_in.shape, BF16), ((1, hid), F32), (w_out.shape, BF16),
                ((hid, CHUNK), F32), (part, F32), (part, BF16), (part, BF16), (half_thin, F32),
                ((3, max(steps, 3)), None), ((3, steps), None),
            ],
            grid_mul * hid, field, mlp_in, mlp_bias[None], w_out, after, *carried,
            first=first, count=half, carried=len(carried),
        )

    hidden_a, slope_a, base_a, weights, forward, inverse = hidden_half(
        0, w_out, spectral_weight, forward, inverse
    )
    wx, zx = call(
        mix_kernel, "vwww", [("w", small, BF16), ("h", modes, F32)],
        [(modes, F32), small_rows, ((1,), None)],
        1 << 24, xp, weights, forward, inverse, sizes=sizes,
    )
    wx = exchange(wx)
    hidden_b, slope_b, base_b = hidden_half(half, zx)
    gp, hidden_gb = call(
        gpre_kernel, "vhhhhhhhhhhh", [("w", large, BF16), ("h", tall, BF16)],
        [
            (thin, BF16), (thin, BF16), (tall, BF16), (tall, BF16), (thin, F32), table, table,
            (w_out.shape, BF16), (thin, BF16), (tall, BF16),
            ((count * chans, 2 * n_phi_modes), BF16), ((half * hid, half * chans), BF16),
            (thin, F32), (tall, F32), small_rows, large_rows, ((hid, LANES), F32),
            ((3, 5), None), ((2,), None),
        ],
        grid_mul * (4 * n_phi_modes + 4 * hid), wx, field, cot,
        hidden_a, hidden_b, slope_a, slope_b, base_a, base_b, phi_fwd, phi_inv, w_out, sizes=sizes,
    )
    gp = exchange(gp)
    partial, inverse_phi = call(
        mlp_grad_kernel, "hhhh", [("w", thin, F32), ("w", phi_inv.shape, BF16)],
        [(thin, BF16), (tall, BF16), (mlp_in.shape, BF16), ((6,), None)],
        grid_mul * hid, cot, hidden_gb, mlp_in, phi_inv, count=half,
    )
    wb, zg = call(
        back_kernel, "vwwww", [("w", large, BF16), ("h", modes, F32)],
        [(modes, F32), large_rows, ((1,), None)],
        1 << 24, gp, weights, forward, inverse, partial, sizes=sizes, each=each,
    )
    wb = exchange(wb)
    factor = math.sqrt(n_phi * n_eta / (n_phi_modes * n_eta_modes))
    grad_shape = (2, owned, n_eta_modes, chans * chans)
    (grad_spectral,) = call(
        weight_grad_kernel, "hh", [("h", grad_shape, F32)],
        [(modes, F32), (modes, F32), (grad_shape, F32), ((2 + 2 * owned,), None)],
        1 << 24, zx, zg, sizes=sizes, factor=factor,
    )
    norm = 1.0 / math.sqrt(layers * depth * n_eta * n_phi)
    grad_in, total_in, total_out, total_bias = call(
        final_kernel, "vwwh",
        [("h", thin, F32), ("h", (chans, hid), F32), ("h", (chans, hid), F32), ("h", (1, hid), F32)],
        [
            (thin, F32), large_rows, ((hid, LANES), F32), ((LANES, hid), F32), ((2, 4), None),
        ],
        grid_mul * 2 * n_phi_modes, wb, partial, inverse_phi, grad_spectral, sizes=sizes, norm=norm,
    )
    if depth > 1:
        grad_spectral = lax.psum_scatter(grad_spectral, "depth", scatter_dimension=2, tiled=True)
        total_in, total_out, total_bias = lax.psum((total_in, total_out, total_bias), "depth")
    return (grad_in.reshape(field_in.shape), grad_spectral, total_in, total_out.T, total_bias[0])


def solution(mesh):
    return jax.shard_map(
        local,
        mesh=mesh,
        in_specs=(
            P("depth", "eta", None, None),
            P("depth", "eta", None, None),
            P(None, "eta", None, None),
            P(),
            P(),
            P(),
        ),
        out_specs=(P("depth", "eta", None, None), P(None, "eta", "depth", None), P(), P(), P()),
        check_vma=False,
    )
```

time: 586 us -> 64 us (0.11)
  waiting for transfers between devices: 338 us -> 18 us
  matrix products: 99.3 us -> 0 us
  local copies, waits for them, and re-layouts: 74.2 us -> 0.65 us
  blocking collectives: 38.8 us -> 0 us
  Pallas kernels: 0 us -> 28.5 us
  starting transfers between devices: 0.8 us -> 15.6 us
  between operations: 14.8 us -> 0.74 us
  other arithmetic: 13.4 us -> 0 us
    reduce_scatter x2 -> x0, waiting for transfers between devices: 277 us -> none  [to_modes(): lax.psum_scatter(eta_forward(spectra, eta_cos, eta_sin), 'eta', scatter_d...]
    dot_general x38 -> x0, matrix products: 99.3 us -> none  [the longest x1 10.8 us: local(): jnp.einsum('decp,ch->dehp', field_in, mlp_in, preferred_element_type=f32)]
    all_gather x2 -> x0, waiting for transfers between devices: 61.8 us -> none  [from_modes(): lax.all_gather(modes, 'eta', axis=0, tiled=True)]
    squeeze x8 -> x0, local copies, waits for them, and re-layouts: 42 us -> none  [the longest x4 27.2 us: eta_inverse(): vi = modes[:, :, 1]]
    psum x1 -> x0, blocking collectives: 38.8 us -> none  [local(): lax.psum((part_in, part_out, part_bias), ('depth', 'eta'))]
    pallas_call x0 -> x9, Pallas kernels: none -> 28.5 us  [call(): pl.pallas_call(functools.partial(kernel, **static), out_shape=[keep[o[0]]...]
    all_to_all x0 -> x4, waiting for transfers between devices: none -> 18 us  [local(): exchange = lambda x: lax.all_to_all(x, 'eta', 0, 0, tiled=True)]
    all_to_all x0 -> x4, starting transfers between devices: none -> 15.6 us  [local(): exchange = lambda x: lax.all_to_all(x, 'eta', 0, 0, tiled=True)]
  transfers between devices with their start and end apart: 4 -> 4, of which waited for: 4 -> 4; matrix products, arithmetic and copies ran while one was open for 9% -> 0% of each run, Pallas kernels for 0% -> 21%
where the time goes in v1:
time: 64 us; the launch traced here: 63.4 us
  Pallas kernels  28.5 us (45%)
  waiting for transfers between devices  18 us (28%)
  starting transfers between devices  15.6 us (24%)
  between operations  0.74 us (1%)
  local copies, waits for them, and re-layouts  0.65 us (1%)
    pallas_call x9, Pallas kernels, call(): pl.pallas_call(functools.partial(kernel, **static), out_shape=[keep[o[0]]...  28.5 us
    all_to_all x4, waiting for transfers between devices, local(): exchange = lambda x: lax.all_to_all(x, 'eta', 0, 0, tiled=True)  18 us
    all_to_all x4, starting transfers between devices, local(): exchange = lambda x: lax.all_to_all(x, 'eta', 0, 0, tiled=True)  15.6 us
  transfers between devices with their start and end apart: 4, of which 4 were waited for; matrix products, arithmetic and copies ran while one was open for 0% of the time, Pallas kernels for 21%

profile of v1, /device:TPU:0, one launch (start us, length us, event | category | flops | bytes accessed | tf_op | source)
XLA Modules:
  0.0 63.4 jit_solution(14916520628190246374)
XLA Ops:
  0.6 2.7 %shard_map.137 = bf16[32,8,128]{2,1,0:T(8,128)(2,1)} custom-call(bf16[256,2048]{1,0:T(8,128)(2,1)} %bitcast.7, bf16[128,2048]{1,0:T(8,128)(2,1)} %constant.8.clone.fwd_h), custom_call_target="tpu_custom_call" | custom-call | flops 134217728 | bytes 1638400 | tf_op jit(solution)/shard_map/pallas_call | solution.py:524
  3.3 7.3 %all-to-all-start = ((bf16[32,8,128]{2,1,0:T(8,128)(2,1)}), bf16[32,8,128]{2,1,0:T(8,128)(2,1)S(1)}, u32[]{:S(2)}, u32[]{:S(2)}) async-start(bf16[32,8,128]{2,1,0:T(8,128)(2,1)} %shard_map.137), calls=%async_computation | async-start | bytes 131072 | tf_op jit(solution)/shard_map/all_to_all | solution.py:570
  10.6 4.4 %shard_map.138 = (bf16[256,2048]{1,0:T(8,128)(2,1)}, bf16[256,2048]{1,0:T(8,128)(2,1)}, f32[128,2048]{1,0:T(8,128)}, bf16[2,2,64,1024]{3,2,1,0:T(8,128)(2,1)S(1)...) custom-call(bf16[256,2048]{1,0:T(8,128)(2,1)} %bitcast.8, bf16[32,64]{1,0:T(8,128)(2,1)} %w_in_h.5, ...), custom_call_target="tpu_custom_call" | custom-call | flops 67108864 | bytes 5714176 | tf_op jit(solution)/shard_map/pallas_call | solution.py:524
  15.0 3.0 %all-to-all-done.blocks = bf16[32,8,128]{2,1,0:T(8,128)(2,1)S(1)} async-done(((bf16[32,8,128]{2,1,0:T(8,128)(2,1)}), bf16[32,8,128]{2,1,0:T(8,128)(2,1)S(1)}, u32[]{:S(2)}, u32[]{:S(2)}) %all-to-all-start) | async-done | bytes 65568 | tf_op jit(solution)/shard_map/all_to_all | solution.py:570
  18.0 2.3 %shard_map.139 = (bf16[32,8,128]{2,1,0:T(8,128)(2,1)}, f32[128,128]{1,0:T(8,128)}) custom-call(bf16[32,8,128]{2,1,0:T(8,128)(2,1)S(1)} %all-to-all-done.blocks, bf16[2,2,64,1024]{3,2,1,0:T(8,128)(2,1)S(1)} %get-tuple-element.26.weights, bf16[128,128]{1,0:T(8,128)(2,1)S(1)} %get-tuple-element.27.forward, bf16[256,384]{1,0:T(8,128)(2,1)S(1)} %get-tuple-element.28.inverse), custom_call_target="tpu_custom_call" | custom-call | flops 16777216 | bytes 950272 | tf_op jit(solution)/shard_map/pallas_call | solution.py:524
  20.3 2.8 %all-to-all-start.1 = ((bf16[32,8,128]{2,1,0:T(8,128)(2,1)}), bf16[32,8,128]{2,1,0:T(8,128)(2,1)S(1)}, u32[]{:S(2)}, u32[]{:S(2)}) async-start(bf16[32,8,128]{2,1,0:T(8,128)(2,1)} %get-tuple-element.29), calls=%async_computation.1 | async-start | bytes 131072 | tf_op jit(solution)/shard_map/all_to_all | solution.py:570
  23.2 4.4 %shard_map.140 = (bf16[256,2048]{1,0:T(8,128)(2,1)}, bf16[256,2048]{1,0:T(8,128)(2,1)}, f32[128,2048]{1,0:T(8,128)}) custom-call(bf16[256,2048]{1,0:T(8,128)(2,1)} %bitcast.9, bf16[32,64]{1,0:T(8,128)(2,1)} %w_in_h.5, f32[1,64]{1,0:T(1,128)} %bitcast.18, bf16[32,64]{1,0:T(8,128)(2,1)} %bitcast.15, f32[128,128]{1,0:T(8,128)} %get-tuple-element.31._.zx_h), custom_call_target="tpu_custom_call" | custom-call | flops 67108864 | bytes 4268288 | tf_op jit(solution)/shard_map/pallas_call | solution.py:524
  27.6 3.0 %all-to-all-done.1.blocks = bf16[32,8,128]{2,1,0:T(8,128)(2,1)S(1)} async-done(((bf16[32,8,128]{2,1,0:T(8,128)(2,1)}), bf16[32,8,128]{2,1,0:T(8,128)(2,1)S(1)}, u32[]{:S(2)}, u32[]{:S(2)}) %all-to-all-start.1) | async-done | bytes 65568 | tf_op jit(solution)/shard_map/all_to_all | solution.py:570
  30.6 6.9 %shard_map.141 = (bf16[32,16,128]{2,1,0:T(8,128)(2,1)}, bf16[512,2048]{1,0:T(8,128)(2,1)}) custom-call(bf16[32,8,128]{2,1,0:T(8,128)(2,1)S(1)} %all-to-all-done.1.blocks, bf16[256,2048]{1,0:T(8,128)(2,1)} %bitcast.10, bf16[256,2048]{1,0:T(8,128)(2,1)} %bitcast.11, bf16[256,2048]{1,0:T(8,128)(2,1)} %get-tuple-element.30.hidden_a, ...), custom_call_target="tpu_custom_call" | custom-call | flops 536870912 | bytes 11735040 | tf_op jit(solution)/shard_map/pallas_call | solution.py:524
  37.5 2.9 %all-to-all-start.2 = ((bf16[32,16,128]{2,1,0:T(8,128)(2,1)}), bf16[32,16,128]{2,1,0:T(8,128)(2,1)S(1)}, u32[]{:S(2)}, u32[]{:S(2)}) async-start(bf16[32,16,128]{2,1,0:T(8,128)(2,1)} %get-tuple-element.37), calls=%async_computation.2 | async-start | bytes 262144 | tf_op jit(solution)/shard_map/all_to_all | solution.py:570
  40.4 2.2 %shard_map.142 = (f32[256,2048]{1,0:T(8,128)S(1)}, bf16[128,2048]{1,0:T(8,128)(2,1)S(1)}) custom-call(bf16[256,2048]{1,0:T(8,128)(2,1)} %bitcast.12, bf16[512,2048]{1,0:T(8,128)(2,1)} %get-tuple-element.38.grad_h, bf16[32,64]{1,0:T(8,128)(2,1)} %w_in_h.5, bf16[128,2048]{1,0:T(8,128)(2,1)} %constant.9.clone.inv_h), custom_call_target="tpu_custom_call" | custom-call | flops 67108864 | bytes 6295552 | tf_op jit(solution)/shard_map/pallas_call | solution.py:524
  42.6 6.0 %all-to-all-done.2.blocks = bf16[32,16,128]{2,1,0:T(8,128)(2,1)S(1)} async-done(((bf16[32,16,128]{2,1,0:T(8,128)(2,1)}), bf16[32,16,128]{2,1,0:T(8,128)(2,1)S(1)}, u32[]{:S(2)}, u32[]{:S(2)}) %all-to-all-start.2) | async-done | bytes 131104 | tf_op jit(solution)/shard_map/all_to_all | solution.py:570
  48.6 1.6 %shard_map.143 = (bf16[32,16,128]{2,1,0:T(8,128)(2,1)S(1)}, f32[128,128]{1,0:T(8,128)}) custom-call(bf16[32,16,128]{2,1,0:T(8,128)(2,1)S(1)} %all-to-all-done.2.blocks, bf16[2,2,64,1024]{3,2,1,0:T(8,128)(2,1)S(1)} %get-tuple-element.26.weights, bf16[128,128]{1,0:T(8,128)(2,1)S(1)} %get-tuple-element.27.forward, ...), custom_call_target="tpu_custom_call" | custom-call | flops 16777216 | bytes 3178496 | tf_op jit(solution)/shard_map/pallas_call | solution.py:524
  50.2 0.0 copy-start
  50.2 0.6 %copy-done = bf16[32,16,128]{2,1,0:T(8,128)(2,1)} copy-done((bf16[32,16,128]{2,1,0:T(8,128)(2,1)}, bf16[32,16,128]{2,1,0:T(8,128)(2,1)S(1)}, u32[]{:S(2)}) %copy-start) | copy-done | bytes 131096
  50.8 2.6 %all-to-all-start.3 = ((bf16[32,16,128]{2,1,0:T(8,128)(2,1)}), bf16[32,16,128]{2,1,0:T(8,128)(2,1)S(1)}, u32[]{:S(2)}, u32[]{:S(2)}) async-start(bf16[32,16,128]{2,1,0:T(8,128)(2,1)} %copy-done), calls=%async_computation.3 | async-start | bytes 262144 | tf_op jit(solution)/shard_map/all_to_all | solution.py:570
  53.4 2.2 %shard_map.144._ = f32[2,2,64,1024]{3,2,1,0:T(8,128)} custom-call(f32[128,128]{1,0:T(8,128)} %get-tuple-element.31._.zx_h, f32[128,128]{1,0:T(8,128)} %get-tuple-element.42.zg_h), custom_call_target="tpu_custom_call" | custom-call | flops 16777216 | bytes 1179648 | tf_op jit(solution)/shard_map/pallas_call | solution.py:524
  55.7 6.0 %all-to-all-done.3.blocks = bf16[32,16,128]{2,1,0:T(8,128)(2,1)S(1)} async-done(((bf16[32,16,128]{2,1,0:T(8,128)(2,1)}), bf16[32,16,128]{2,1,0:T(8,128)(2,1)S(1)}, u32[]{:S(2)}, u32[]{:S(2)}) %all-to-all-start.3) | async-done | bytes 131104 | tf_op jit(solution)/shard_map/all_to_all | solution.py:570
  61.7 1.8 %shard_map.145 = (f32[256,2048]{1,0:T(8,128)}, f32[32,64]{1,0:T(8,128)}, f32[32,64]{1,0:T(8,128)}, f32[1,64]{1,0:T(1,128)}) custom-call(bf16[32,16,128]{2,1,0:T(8,128)(2,1)S(1)} %all-to-all-done.3.blocks, f32[256,2048]{1,0:T(8,128)S(1)} %get-tuple-element.39._.base, bf16[128,2048]{1,0:T(8,128)(2,1)S(1)} %get-tuple-element.41.inv, ...), custom_call_target="tpu_custom_call" | custom-call | flops 134217728 | bytes 5914880 | tf_op jit(solution)/shard_map/pallas_call | solution.py:524
Async XLA Ops:
  3.3 14.7 %all-to-all-start = ((bf16[32,8,128]{2,1,0:T(8,128)(2,1)}), bf16[32,8,128]{2,1,0:T(8,128)(2,1)S(1)}, u32[]{:S(2)}, u32[]{:S(2)}) async-start(bf16[32,8,128]{2,1,0:T(8,128)(2,1)} %shard_map.137), calls=%async_computation | async-start | bytes 131072 | tf_op jit(solution)/shard_map/all_to_all | solution.py:570
  20.3 10.2 %all-to-all-start.1 = ((bf16[32,8,128]{2,1,0:T(8,128)(2,1)}), bf16[32,8,128]{2,1,0:T(8,128)(2,1)S(1)}, u32[]{:S(2)}, u32[]{:S(2)}) async-start(bf16[32,8,128]{2,1,0:T(8,128)(2,1)} %get-tuple-element.29), calls=%async_computation.1 | async-start | bytes 131072 | tf_op jit(solution)/shard_map/all_to_all | solution.py:570
  37.5 11.1 %all-to-all-start.2 = ((bf16[32,16,128]{2,1,0:T(8,128)(2,1)}), bf16[32,16,128]{2,1,0:T(8,128)(2,1)S(1)}, u32[]{:S(2)}, u32[]{:S(2)}) async-start(bf16[32,16,128]{2,1,0:T(8,128)(2,1)} %get-tuple-element.37), calls=%async_computation.2 | async-start | bytes 262144 | tf_op jit(solution)/shard_map/all_to_all | solution.py:570
  50.2 0.7 %copy-start = (bf16[32,16,128]{2,1,0:T(8,128)(2,1)}, bf16[32,16,128]{2,1,0:T(8,128)(2,1)S(1)}, u32[]{:S(2)}) copy-start(bf16[32,16,128]{2,1,0:T(8,128)(2,1)S(1)} %get-tuple-element.40) | copy-start | bytes 393220
  50.8 10.8 %all-to-all-start.3 = ((bf16[32,16,128]{2,1,0:T(8,128)(2,1)}), bf16[32,16,128]{2,1,0:T(8,128)(2,1)S(1)}, u32[]{:S(2)}, u32[]{:S(2)}) async-start(bf16[32,16,128]{2,1,0:T(8,128)(2,1)} %copy-done), calls=%async_computation.3 | async-start | bytes 262144 | tf_op jit(solution)/shard_map/all_to_all | solution.py:570

commit v2 on v1

--- a/solution.py
+++ b/solution.py
@@ -112,9 +112,11 @@
             rows_ref[pl.ds(cell * 2 + part, owners, rows), :] = jnp.concatenate(pieces, axis=1)
 
 
-def xp_kernel(field_h, fwd_h, out, field, fwd, rows_ref, sems, *, sizes):
+def xp_kernel(fwd_h, field_h, *refs, sizes):
     layers, cells, owners, owned = sizes
-    copies = [load(fwd_h, fwd, sems.at[0]), load(field_h, field, sems.at[1])]
+    smalls, out, field, targets, (fwd, rows_ref, sems) = refs[:3], refs[3], refs[4], refs[5:8], refs[8:]
+    pairs = ((fwd_h, fwd), (field_h, field), *zip(smalls, targets))
+    copies = [load(a, b, sems.at[n]) for n, (a, b) in enumerate(pairs)]
     for copy in copies:
         copy.start()
     for copy in copies:
@@ -131,41 +133,33 @@
     return jnp.where(same, wide, 0.0).astype(BF16)
 
 
-def hidden_kernel(field_h, w_in_h, bias_h, w_out_h, _, *refs, first, count, carried):
+def hidden_kernel(field, w_in, bias, w_out, _, *refs, first, count, carried):
     sources, (hidden_h, slope_h, base_h), refs = refs[:carried], refs[carried : carried + 3], refs[carried + 3 :]
     targets, refs = refs[:carried], refs[carried:]
-    field, w_in, bias, w_out, wide_bias, pre, hidden, slope, base, ins, outs = refs
-    carries = [load(a, b, ins.at[2, n]) for n, (a, b) in enumerate(zip(sources, targets))]
+    wide_bias, pre, hidden, slope, ins, outs, *own = refs
+    base = own[0] if own else base_h
+    carries = [load(a, b, ins.at[n]) for n, (a, b) in enumerate(zip(sources, targets))]
+    for copy in carries:
+        copy.start()
     steps = field.shape[1] // STEP
     chans, hid = w_in.shape
-    smalls = ((w_in_h, w_in), (bias_h, bias), (w_out_h, w_out))
-    small = [load(a, b, ins.at[1, n]) for n, (a, b) in enumerate(smalls)]
-    for copy in small:
-        copy.start()
     rows = pl.ds(first * chans, count * chans)
     span = lambda j: pl.ds(j * STEP, STEP)
-    read = lambda j: load(field_h.at[rows, span(j)], field.at[:, span(j)], ins.at[0, j])
     pairs = ((hidden, hidden_h), (slope, slope_h), (base, base_h))
     write = lambda n, j: load(
         pairs[n][0].at[:, span(j)], pairs[n][1].at[:, span(j)], outs.at[n, j]
     )
-    for j in range(steps):
-        read(j).start()
-    for copy in carries:
-        copy.start()
-    for copy in small:
-        copy.wait()
     wide = by_cell(w_in[...].astype(F32).T, count)
     back = by_cell(w_out[...].astype(F32), count)
     wide_bias[...] = jnp.broadcast_to(bias[...].T, wide_bias.shape)
 
     def project(j):
         base[:, span(j)] = dot(back, hidden[:, span(j)])
-        write(2, j).start()
+        if own:
+            write(2, j).start()
 
     for j in range(steps):
-        read(j).wait()
-        pre[:, span(j)] = dot(wide, field[:, span(j)])
+        pre[:, span(j)] = dot(wide, field[rows, span(j)])
         if j:
             project(j - 1)
         for left in range(j * STEP, (j + 1) * STEP, CHUNK):
@@ -180,7 +174,7 @@
             write(n, j).start()
     project(steps - 1)
     for j in range(steps):
-        for n in range(3):
+        for n in range(3 if own else 2):
             write(n, j).wait()
     for copy in carries:
         copy.wait()
@@ -272,9 +266,9 @@
 
 
 def gpre_kernel(
-    blocks, field_h, cot_h, hidden_a, hidden_b, slope_a, slope_b, base_a, base_b,
-    fwd_h, inv_h, w_out_h, out, grad_h,
-    field, cot, hidden, slope, base, fwd, inv, w_out, gpre, grad_b, waves, back, pre, grad,
+    blocks, cot, base_a, inv, w_out, field_h, hidden_a, hidden_b, slope_a, slope_b, base_h,
+    fwd_h, out, grad_h,
+    field, hidden, slope, base_b, fwd, gpre, grad_b, waves, back, pre, grad,
     rows_in, rows_out, slab, ins, outs, *, sizes,
 ):
     layers, cells, owners, owned = sizes
@@ -284,29 +278,23 @@
     count = thin // chans
     rows = lambda n: pl.ds(n * thin, thin)
     high = lambda n: pl.ds(n * tall, tall)
-    whole = [load(a, b, ins.at[0, n]) for n, (a, b) in enumerate(((w_out_h, w_out), (inv_h, inv), (fwd_h, fwd)))]
-    early = [
-        [
-            load((base_a, base_b)[n], base.at[rows(n), :], ins.at[1 + n, 0]),
-            load(cot_h.at[rows(n), :], cot.at[rows(n), :], ins.at[1 + n, 1]),
-            load((slope_a, slope_b)[n], slope.at[high(n), :], ins.at[1 + n, 2]),
-        ]
-        for n in range(2)
+    bases = (base_a, base_b)
+    others = [load(fwd_h, fwd, ins.at[2, 0]), load(base_h, base_b, ins.at[2, 1])]
+    slopes = [
+        load((slope_a, slope_b)[n], slope.at[high(n), :], ins.at[n, 0]) for n in range(2)
     ]
     late = [
         [
-            load((hidden_a, hidden_b)[n], hidden.at[high(n), :], ins.at[1 + n, 3]),
-            load(field_h.at[rows(n), :], field.at[rows(n), :], ins.at[1 + n, 4]),
+            load((hidden_a, hidden_b)[n], hidden.at[high(n), :], ins.at[n, 1]),
+            load(field_h.at[rows(n), :], field.at[rows(n), :], ins.at[n, 2]),
         ]
         for n in range(2)
     ]
     writes = [load(grad_b.at[high(n), :], grad_h.at[high(n), :], outs.at[n]) for n in range(2)]
-    for copy in (*whole[:2], *early[0], *early[1], whole[2], *late[0], *late[1]):
+    for copy in (slopes[0], others[1], others[0], *late[0], slopes[1], *late[1]):
         copy.start()
     waves[...] = phi_rows(blocks, rows_in, layers, cells, owners, owned)
-    whole[0].wait()
     back[...] = by_cell(w_out[...].astype(F32).T, count)
-    whole[1].wait()
 
     def products(n):
         here, up = slice(n * thin, (n + 1) * thin), slice(n * tall, (n + 1) * tall)
@@ -323,20 +311,21 @@
     for n in range(2):
         here, up = slice(n * thin, (n + 1) * thin), slice(n * tall, (n + 1) * tall)
         pre[here, :] = dot(waves[here, :], inv[...])
-        for copy in early[n]:
-            copy.wait()
         if n:
-            for copy in (whole[2], *late[0]):
+            for copy in (*others, *late[0], slopes[1]):
                 copy.wait()
             results.append(products(0))
         for left in range(0, n_phi, CHUNK):
             at = slice(left, left + CHUNK)
             for top in range(here.start, here.stop, hid):
                 tile = slice(top, top + hid)
-                g = 0.5 + gelu_parts(pre[tile, at] + base[tile, at])[1]
+                base = bases[n][top - here.start : top - here.start + hid, at]
+                g = 0.5 + gelu_parts(pre[tile, at] + base)[1]
                 gpre[tile, at] = (cot[tile, at].astype(F32) * g).astype(BF16)
         for left in range(0, n_phi, STEP):
             grad[up, left : left + STEP] = dot(back[...], gpre[here, left : left + STEP])
+        if n == 0:
+            slopes[0].wait()
         for left in range(0, n_phi, CHUNK):
             at = slice(left, left + CHUNK)
             for top in range(up.start, up.stop, hid):
@@ -576,53 +565,55 @@
     table = ((2 * n_phi_modes, n_phi), BF16)
     grid_mul = 2 * count * n_phi * chans
 
-    (xp,) = call(
-        xp_kernel, "hh", [("w", small, BF16)],
-        [(thin, BF16), table, small_rows, ((2,), None)],
-        grid_mul * 2 * n_phi_modes, field, phi_fwd, sizes=sizes,
+    smalls = (mlp_in, mlp_bias[None], w_out)
+    xp, field_v, w_in_v, bias_v, w_out_v = call(
+        xp_kernel, "hhhhh",
+        [("v", small, BF16), ("w", thin, BF16), *(("w", x.shape, x.dtype) for x in smalls)],
+        [table, small_rows, ((5,), None)],
+        grid_mul * 2 * n_phi_modes, phi_fwd, field, *smalls, sizes=sizes,
     )
     xp = exchange(xp)
     half = count // 2
     part = (half * hid, n_phi)
     half_thin = (half * chans, n_phi)
 
-    def hidden_half(first, after, *carried):
+    def hidden_half(first, after, keep_base, *carried):
         return call(
-            hidden_kernel, "hhhhh" + "h" * len(carried),
+            hidden_kernel, "wwwwh" + "h" * len(carried),
             [
-                ("h", part, BF16), ("h", part, BF16), ("h", half_thin, F32),
+                ("h", part, BF16), ("h", part, BF16), (keep_base, half_thin, F32),
                 *(("w", x.shape, x.dtype) for x in carried),
             ],
             [
-                (half_thin, BF16), (mlp_in.shape, BF16), ((1, hid), F32), (w_out.shape, BF16),
-                ((hid, CHUNK), F32), (part, F32), (part, BF16), (part, BF16), (half_thin, F32),
-                ((3, max(steps, 3)), None), ((3, steps), None),
+                ((hid, CHUNK), F32), (part, F32), (part, BF16), (part, BF16),
+                ((len(carried),), None), ((3, steps), None),
+                *([(half_thin, F32)] if keep_base == "h" else []),
             ],
-            grid_mul * hid, field, mlp_in, mlp_bias[None], w_out, after, *carried,
+            grid_mul * hid, field_v, w_in_v, bias_v, w_out_v, after, *carried,
             first=first, count=half, carried=len(carried),
         )
 
     hidden_a, slope_a, base_a, weights, forward, inverse = hidden_half(
-        0, w_out, spectral_weight, forward, inverse
+        0, w_out, "w", spectral_weight, forward, inverse
     )
     wx, zx = call(
-        mix_kernel, "vwww", [("w", small, BF16), ("h", modes, F32)],
+        mix_kernel, "vwww", [("v", small, BF16), ("h", modes, F32)],
         [(modes, F32), small_rows, ((1,), None)],
         1 << 24, xp, weights, forward, inverse, sizes=sizes,
     )
     wx = exchange(wx)
-    hidden_b, slope_b, base_b = hidden_half(half, zx)
+    hidden_b, slope_b, base_b, cot_v, inv_v = hidden_half(half, zx, "h", cot, phi_inv)
     gp, hidden_gb = call(
-        gpre_kernel, "vhhhhhhhhhhh", [("w", large, BF16), ("h", tall, BF16)],
+        gpre_kernel, "vwwwwhhhhhhh", [("v", large, BF16), ("h", tall, BF16)],
         [
-            (thin, BF16), (thin, BF16), (tall, BF16), (tall, BF16), (thin, F32), table, table,
-            (w_out.shape, BF16), (thin, BF16), (tall, BF16),
+            (thin, BF16), (tall, BF16), (tall, BF16), (half_thin, F32), table,
+            (thin, BF16), (tall, BF16),
             ((count * chans, 2 * n_phi_modes), BF16), ((half * hid, half * chans), BF16),
             (thin, F32), (tall, F32), small_rows, large_rows, ((hid, LANES), F32),
-            ((3, 5), None), ((2,), None),
+            ((3, 3), None), ((2,), None),
         ],
-        grid_mul * (4 * n_phi_modes + 4 * hid), wx, field, cot,
-        hidden_a, hidden_b, slope_a, slope_b, base_a, base_b, phi_fwd, phi_inv, w_out, sizes=sizes,
+        grid_mul * (4 * n_phi_modes + 4 * hid), wx, cot_v, base_a, inv_v, w_out_v,
+        field, hidden_a, hidden_b, slope_a, slope_b, base_b, phi_fwd, sizes=sizes,
     )
     gp = exchange(gp)
     partial, inverse_phi = call(

time: 64 us -> 64.5 us (level)
  Pallas kernels: 28.5 us -> 25.8 us
  local copies, waits for them, and re-layouts: 0.65 us -> 2.84 us
  waiting for transfers between devices: 18 us -> 18.9 us
    pallas_call x9, Pallas kernels: 28.5 us -> 25.8 us  [call(): pl.pallas_call(functools.partial(kernel, **static), out_shape=[keep[o[0]]...]
    unnamed x2 -> x6, local copies, waits for them, and re-layouts: 0.65 us -> 2.84 us
    all_to_all x4, waiting for transfers between devices: 18 us -> 18.9 us  [local(): exchange = lambda x: lax.all_to_all(x, 'eta', 0, 0, tiled=True)]
  transfers between devices with their start and end apart: 4 -> 4, of which waited for: 4 -> 4; matrix products, arithmetic and copies ran while one was open for 0% -> 0% of each run, Pallas kernels for 21% -> 18%
where the time goes in v2:
time: 64.5 us; the launch traced here: 64 us
  Pallas kernels  25.8 us (40%)
  waiting for transfers between devices  18.9 us (29%)
  starting transfers between devices  15.6 us (24%)
  local copies, waits for them, and re-layouts  2.84 us (4%)
  between operations  0.75 us (1%)
    pallas_call x9, Pallas kernels, call(): pl.pallas_call(functools.partial(kernel, **static), out_shape=[keep[o[0]]...  25.8 us
    all_to_all x4, waiting for transfers between devices, local(): exchange = lambda x: lax.all_to_all(x, 'eta', 0, 0, tiled=True)  18.9 us
    all_to_all x4, starting transfers between devices, local(): exchange = lambda x: lax.all_to_all(x, 'eta', 0, 0, tiled=True)  15.6 us
    unnamed x6, local copies, waits for them, and re-layouts  2.84 us
  transfers between devices with their start and end apart: 4, of which 4 were waited for; matrix products, arithmetic and copies ran while one was open for 0% of the time, Pallas kernels for 18%

profile of v2, /device:TPU:0, one launch (start us, length us, event | category | flops | bytes accessed | tf_op | source)
XLA Modules:
  0.0 64.0 jit_solution(9448678236436538311)
XLA Ops:
  0.6 2.7 %shard_map.137 = (bf16[32,8,128]{2,1,0:T(8,128)(2,1)}, bf16[256,2048]{1,0:T(8,128)(2,1)S(1)}, bf16[32,64]{1,0:T(8,128)(2,1)S(1)}, f32[1,64]{1,0:T(1,128)S(1)}, bf16[32,64]{1,0:T(8,128)(2,1)S(1)}) custom-call(bf16[128,2048]{1,0:T(8,128)(2,1)} %constant.8.clone.fwd_h, bf16[256,2048]{1,0:T(8,128)(2,1)} %bitcast.9, bf16[32,64]{1,0:T(8,128)(2,1)} %w_in_h.1, ...), custom_call_target="tpu_custom_call" | custom-call | flops 134217728 | bytes 2703872 | tf_op jit(solution)/shard_map/pallas_call | solution.py:513
  3.3 7.3 %all-to-all-start = ((bf16[32,8,128]{2,1,0:T(8,128)(2,1)}), bf16[32,8,128]{2,1,0:T(8,128)(2,1)S(1)}, u32[]{:S(2)}, u32[]{:S(2)}) async-start(bf16[32,8,128]{2,1,0:T(8,128)(2,1)} %get-tuple-element.33), calls=%async_computation | async-start | bytes 131072 | tf_op jit(solution)/shard_map/all_to_all | solution.py:559
  10.7 3.1 %shard_map.138 = (bf16[256,2048]{1,0:T(8,128)(2,1)}, bf16[256,2048]{1,0:T(8,128)(2,1)}, f32[128,2048]{1,0:T(8,128)S(1)}, bf16[2,2,64,1024]{3,2,1,0:T(8,128)(2,1)...) custom-call(bf16[256,2048]{1,0:T(8,128)(2,1)S(1)} %get-tuple-element.34.field, ...), custom_call_target="tpu_custom_call" | custom-call | flops 67108864 | bytes 5714176 | tf_op jit(solution)/shard_map/pallas_call | solution.py:513
  13.7 4.3 %all-to-all-done.blocks = bf16[32,8,128]{2,1,0:T(8,128)(2,1)S(1)} async-done(((bf16[32,8,128]{2,1,0:T(8,128)(2,1)}), bf16[32,8,128]{2,1,0:T(8,128)(2,1)S(1)}, u32[]{:S(2)}, u32[]{:S(2)}) %all-to-all-start) | async-done | bytes 65568 | tf_op jit(solution)/shard_map/all_to_all | solution.py:559
  18.1 2.3 %shard_map.139 = (bf16[32,8,128]{2,1,0:T(8,128)(2,1)}, f32[128,128]{1,0:T(8,128)}) custom-call(bf16[32,8,128]{2,1,0:T(8,128)(2,1)S(1)} %all-to-all-done.blocks, bf16[2,2,64,1024]{3,2,1,0:T(8,128)(2,1)S(1)} %get-tuple-element.38.weights, bf16[128,128]{1,0:T(8,128)(2,1)S(1)} %get-tuple-element.39.forward, bf16[256,384]{1,0:T(8,128)(2,1)S(1)} %get-tuple-element.40.inverse), custom_call_target="tpu_custom_call" | custom-call | flops 16777216 | bytes 950272 | tf_op jit(solution)/shard_map/pallas_call | solution.py:513
  20.4 2.6 %all-to-all-start.1 = ((bf16[32,8,128]{2,1,0:T(8,128)(2,1)}), bf16[32,8,128]{2,1,0:T(8,128)(2,1)S(1)}, u32[]{:S(2)}, u32[]{:S(2)}) async-start(bf16[32,8,128]{2,1,0:T(8,128)(2,1)} %get-tuple-element.41), calls=%async_computation.1 | async-start | bytes 131072 | tf_op jit(solution)/shard_map/all_to_all | solution.py:559
  23.0 3.8 %shard_map.140 = (bf16[256,2048]{1,0:T(8,128)(2,1)}, bf16[256,2048]{1,0:T(8,128)(2,1)}, f32[128,2048]{1,0:T(8,128)}, bf16[256,2048]{1,0:T(8,128)(2,1)S(1)}, bf16[128,2048]{1,0:T(8,128)(2,1)S(1)}) custom-call(bf16[256,2048]{1,0:T(8,128)(2,1)S(1)} %get-tuple-element.34.field, bf16[32,64]{1,0:T(8,128)(2,1)S(1)} %get-tuple-element.35.w_in, ...), custom_call_target="tpu_custom_call" | custom-call | flops 67108864 | bytes 7414016 | tf_op jit(solution)/shard_map/pallas_call | solution.py:513
  26.7 0.0 copy-start
  26.7 1.0 %copy-done = bf16[256,2048]{1,0:T(8,128)(2,1)} copy-done((bf16[256,2048]{1,0:T(8,128)(2,1)}, bf16[256,2048]{1,0:T(8,128)(2,1)S(1)}, u32[]{:S(2)}) %copy-start) | copy-done | bytes 1048600
  27.7 2.7 %all-to-all-done.1.blocks = bf16[32,8,128]{2,1,0:T(8,128)(2,1)S(1)} async-done(((bf16[32,8,128]{2,1,0:T(8,128)(2,1)}), bf16[32,8,128]{2,1,0:T(8,128)(2,1)S(1)}, u32[]{:S(2)}, u32[]{:S(2)}) %all-to-all-start.1) | async-done | bytes 65568 | tf_op jit(solution)/shard_map/all_to_all | solution.py:559
  30.4 0.0 copy-start.1
  30.4 1.2 %copy-done.1 = bf16[256,2048]{1,0:T(8,128)(2,1)S(1)} copy-done((bf16[256,2048]{1,0:T(8,128)(2,1)S(1)}, bf16[256,2048]{1,0:T(8,128)(2,1)}, u32[]{:S(2)}) %copy-start.1) | copy-done | bytes 1048600
  31.6 6.1 %shard_map.141 = (bf16[32,16,128]{2,1,0:T(8,128)(2,1)}, bf16[512,2048]{1,0:T(8,128)(2,1)}) custom-call(bf16[32,8,128]{2,1,0:T(8,128)(2,1)S(1)} %all-to-all-done.1.blocks, bf16[256,2048]{1,0:T(8,128)(2,1)S(1)} %copy-done.1, f32[128,2048]{1,0:T(8,128)S(1)} %get-tuple-element.44.base_a, bf16[128,2048]{1,0:T(8,128)(2,1)S(1)} %get-tuple-element.45.inv, ...), custom_call_target="tpu_custom_call" | custom-call | flops 536870912 | bytes 11735040 | tf_op jit(solution)/shard_map/pallas_call | solution.py:513
  37.7 3.2 %all-to-all-start.2 = ((bf16[32,16,128]{2,1,0:T(8,128)(2,1)}), bf16[32,16,128]{2,1,0:T(8,128)(2,1)S(1)}, u32[]{:S(2)}, u32[]{:S(2)}) async-start(bf16[32,16,128]{2,1,0:T(8,128)(2,1)} %get-tuple-element.51), calls=%async_computation.2 | async-start | bytes 262144 | tf_op jit(solution)/shard_map/all_to_all | solution.py:559
  40.9 2.2 %shard_map.142 = (f32[256,2048]{1,0:T(8,128)S(1)}, bf16[128,2048]{1,0:T(8,128)(2,1)S(1)}) custom-call(bf16[256,2048]{1,0:T(8,128)(2,1)} %bitcast.8, bf16[512,2048]{1,0:T(8,128)(2,1)} %get-tuple-element.52.grad_h, bf16[32,64]{1,0:T(8,128)(2,1)} %w_in_h.1, bf16[128,2048]{1,0:T(8,128)(2,1)} %constant.9.clone.refs_1_.inv_h), custom_call_target="tpu_custom_call" | custom-call | flops 67108864 | bytes 6295552 | tf_op jit(solution)/shard_map/pallas_call | solution.py:513
  43.2 6.0 %all-to-all-done.2.blocks = bf16[32,16,128]{2,1,0:T(8,128)(2,1)S(1)} async-done(((bf16[32,16,128]{2,1,0:T(8,128)(2,1)}), bf16[32,16,128]{2,1,0:T(8,128)(2,1)S(1)}, u32[]{:S(2)}, u32[]{:S(2)}) %all-to-all-start.2) | async-done | bytes 131104 | tf_op jit(solution)/shard_map/all_to_all | solution.py:559
  49.1 1.6 %shard_map.143 = (bf16[32,16,128]{2,1,0:T(8,128)(2,1)S(1)}, f32[128,128]{1,0:T(8,128)}) custom-call(bf16[32,16,128]{2,1,0:T(8,128)(2,1)S(1)} %all-to-all-done.2.blocks, bf16[2,2,64,1024]{3,2,1,0:T(8,128)(2,1)S(1)} %get-tuple-element.38.weights, bf16[128,128]{1,0:T(8,128)(2,1)S(1)} %get-tuple-element.39.forward, ...), custom_call_target="tpu_custom_call" | custom-call | flops 16777216 | bytes 3178496 | tf_op jit(solution)/shard_map/pallas_call | solution.py:513
  50.7 0.0 copy-start.2
  50.7 0.6 %copy-done.2 = bf16[32,16,128]{2,1,0:T(8,128)(2,1)} copy-done((bf16[32,16,128]{2,1,0:T(8,128)(2,1)}, bf16[32,16,128]{2,1,0:T(8,128)(2,1)S(1)}, u32[]{:S(2)}) %copy-start.2) | copy-done | bytes 131096
  51.4 2.6 %all-to-all-start.3 = ((bf16[32,16,128]{2,1,0:T(8,128)(2,1)}), bf16[32,16,128]{2,1,0:T(8,128)(2,1)S(1)}, u32[]{:S(2)}, u32[]{:S(2)}) async-start(bf16[32,16,128]{2,1,0:T(8,128)(2,1)} %copy-done.2), calls=%async_computation.3 | async-start | bytes 262144 | tf_op jit(solution)/shard_map/all_to_all | solution.py:559
  54.0 2.2 %shard_map.144._ = f32[2,2,64,1024]{3,2,1,0:T(8,128)} custom-call(f32[128,128]{1,0:T(8,128)} %get-tuple-element.42._.zx_h, f32[128,128]{1,0:T(8,128)} %get-tuple-element.56.zg_h), custom_call_target="tpu_custom_call" | custom-call | flops 16777216 | bytes 1179648 | tf_op jit(solution)/shard_map/pallas_call | solution.py:513
  56.2 6.0 %all-to-all-done.3.blocks = bf16[32,16,128]{2,1,0:T(8,128)(2,1)S(1)} async-done(((bf16[32,16,128]{2,1,0:T(8,128)(2,1)}), bf16[32,16,128]{2,1,0:T(8,128)(2,1)S(1)}, u32[]{:S(2)}, u32[]{:S(2)}) %all-to-all-start.3) | async-done | bytes 131104 | tf_op jit(solution)/shard_map/all_to_all | solution.py:559
  62.2 1.8 %shard_map.145 = (f32[256,2048]{1,0:T(8,128)}, f32[32,64]{1,0:T(8,128)}, f32[32,64]{1,0:T(8,128)}, f32[1,64]{1,0:T(1,128)}) custom-call(bf16[32,16,128]{2,1,0:T(8,128)(2,1)S(1)} %all-to-all-done.3.blocks, f32[256,2048]{1,0:T(8,128)S(1)} %get-tuple-element.53._.base, bf16[128,2048]{1,0:T(8,128)(2,1)S(1)} %get-tuple-element.55.inv, ...), custom_call_target="tpu_custom_call" | custom-call | flops 134217728 | bytes 5914880 | tf_op jit(solution)/shard_map/pallas_call | solution.py:513
Async XLA Ops:
  3.3 14.7 %all-to-all-start = ((bf16[32,8,128]{2,1,0:T(8,128)(2,1)}), bf16[32,8,128]{2,1,0:T(8,128)(2,1)S(1)}, u32[]{:S(2)}, u32[]{:S(2)}) async-start(bf16[32,8,128]{2,1,0:T(8,128)(2,1)} %get-tuple-element.33), calls=%async_computation | async-start | bytes 131072 | tf_op jit(solution)/shard_map/all_to_all | solution.py:559
  20.4 10.0 %all-to-all-start.1 = ((bf16[32,8,128]{2,1,0:T(8,128)(2,1)}), bf16[32,8,128]{2,1,0:T(8,128)(2,1)S(1)}, u32[]{:S(2)}, u32[]{:S(2)}) async-start(bf16[32,8,128]{2,1,0:T(8,128)(2,1)} %get-tuple-element.41), calls=%async_computation.1 | async-start | bytes 131072 | tf_op jit(solution)/shard_map/all_to_all | solution.py:559
  26.7 1.0 %copy-start = (bf16[256,2048]{1,0:T(8,128)(2,1)}, bf16[256,2048]{1,0:T(8,128)(2,1)S(1)}, u32[]{:S(2)}) copy-start(bf16[256,2048]{1,0:T(8,128)(2,1)S(1)} %get-tuple-element.43.cot) | copy-start | bytes 3145732
  30.4 1.2 %copy-start.1 = (bf16[256,2048]{1,0:T(8,128)(2,1)S(1)}, bf16[256,2048]{1,0:T(8,128)(2,1)}, u32[]{:S(2)}) copy-start(bf16[256,2048]{1,0:T(8,128)(2,1)} %copy-done) | copy-start | bytes 3145732
  37.7 11.4 %all-to-all-start.2 = ((bf16[32,16,128]{2,1,0:T(8,128)(2,1)}), bf16[32,16,128]{2,1,0:T(8,128)(2,1)S(1)}, u32[]{:S(2)}, u32[]{:S(2)}) async-start(bf16[32,16,128]{2,1,0:T(8,128)(2,1)} %get-tuple-element.51), calls=%async_computation.2 | async-start | bytes 262144 | tf_op jit(solution)/shard_map/all_to_all | solution.py:559
  50.7 0.7 %copy-start.2 = (bf16[32,16,128]{2,1,0:T(8,128)(2,1)}, bf16[32,16,128]{2,1,0:T(8,128)(2,1)S(1)}, u32[]{:S(2)}) copy-start(bf16[32,16,128]{2,1,0:T(8,128)(2,1)S(1)} %get-tuple-element.54) | copy-start | bytes 393220
  51.4 10.8 %all-to-all-start.3 = ((bf16[32,16,128]{2,1,0:T(8,128)(2,1)}), bf16[32,16,128]{2,1,0:T(8,128)(2,1)S(1)}, u32[]{:S(2)}, u32[]{:S(2)}) async-start(bf16[32,16,128]{2,1,0:T(8,128)(2,1)} %copy-done.2), calls=%async_computation.3 | async-start | bytes 262144 | tf_op jit(solution)/shard_map/all_to_all | solution.py:559

commit v3 on v2

--- a/solution.py
+++ b/solution.py
@@ -114,16 +114,23 @@
 
 def xp_kernel(fwd_h, field_h, *refs, sizes):
     layers, cells, owners, owned = sizes
-    smalls, out, field, targets, (fwd, rows_ref, sems) = refs[:3], refs[3], refs[4], refs[5:8], refs[8:]
-    pairs = ((fwd_h, fwd), (field_h, field), *zip(smalls, targets))
+    smalls, out_h, fields, targets, (out, fwd, rows_ref, sems) = refs[:3], refs[3], refs[4:6], refs[6:9], refs[9:]
+    half = fields[0].shape[0]
+    halves = [(field_h.at[pl.ds(n * half, half), :], fields[n]) for n in range(2)]
+    pairs = ((fwd_h, fwd), *halves, *zip(smalls, targets))
     copies = [load(a, b, sems.at[n]) for n, (a, b) in enumerate(pairs)]
     for copy in copies:
         copy.start()
-    for copy in copies:
+    for copy in copies[:3]:
         copy.wait()
-    spectra = dot_rows(fwd[...], field[...])
+    field = jnp.concatenate([fields[0][...], fields[1][...]], axis=0)
+    spectra = dot_rows(fwd[...], field)
     pack_spectra(spectra, rows_ref, 8, layers, cells, owners, owned)
     out[...] = rows_ref[...].reshape(out.shape).astype(BF16)
+    send = load(out, out_h, sems.at[len(copies)])
+    send.start()
+    for copy in (*copies[3:], send):
+        copy.wait()
 
 
 def by_cell(weights, cells):
@@ -133,7 +140,7 @@
     return jnp.where(same, wide, 0.0).astype(BF16)
 
 
-def hidden_kernel(field, w_in, bias, w_out, _, *refs, first, count, carried):
+def hidden_kernel(field, w_in, bias, w_out, _, *refs, count, carried):
     sources, (hidden_h, slope_h, base_h), refs = refs[:carried], refs[carried : carried + 3], refs[carried + 3 :]
     targets, refs = refs[:carried], refs[carried:]
     wide_bias, pre, hidden, slope, ins, outs, *own = refs
@@ -143,7 +150,6 @@
         copy.start()
     steps = field.shape[1] // STEP
     chans, hid = w_in.shape
-    rows = pl.ds(first * chans, count * chans)
     span = lambda j: pl.ds(j * STEP, STEP)
     pairs = ((hidden, hidden_h), (slope, slope_h), (base, base_h))
     write = lambda n, j: load(
@@ -159,7 +165,7 @@
             write(2, j).start()
 
     for j in range(steps):
-        pre[:, span(j)] = dot(wide, field[rows, span(j)])
+        pre[:, span(j)] = dot(wide, field[:, span(j)])
         if j:
             project(j - 1)
         for left in range(j * STEP, (j + 1) * STEP, CHUNK):
@@ -212,7 +218,7 @@
 
 
 def mix_kernel(
-    blocks, weights, forward, inverse, out, modes_h, modes, rows_ref, sems, *, sizes,
+    blocks, weights, forward, inverse, out_h, modes_h, out, modes, rows_ref, sems, *, sizes,
 ):
     layers, cells, owners, owned = sizes
     chans = LANES // (layers * owned)
@@ -246,7 +252,10 @@
     mixed = dot(high, gather) + dot(low, gather)
     fields_of(mixed, inverse, rows_ref, 8, cells, owners)
     out[...] = rows_ref[...].reshape(out.shape).astype(BF16)
+    send = load(out, out_h, sems.at[1])
+    send.start()
     save.wait()
+    send.wait()
 
 
 def phi_rows(blocks, rows_ref, layers, cells, owners, owned):
@@ -267,8 +276,8 @@
 
 def gpre_kernel(
     blocks, cot, base_a, inv, w_out, field_h, hidden_a, hidden_b, slope_a, slope_b, base_h,
-    fwd_h, out, grad_h,
-    field, hidden, slope, base_b, fwd, gpre, grad_b, waves, back, pre, grad,
+    fwd_h, out_h, grad_h,
+    out, field, hidden, slope, base_b, fwd, gpre, grad_b, waves, back, pre, grad,
     rows_in, rows_out, slab, ins, outs, *, sizes,
 ):
     layers, cells, owners, owned = sizes
@@ -353,11 +362,15 @@
     for row in range(8 + 2 * each, 16):
         rows_out[pl.ds(row, owners, 16), :] = jnp.zeros((owners, LANES), F32)
     out[...] = rows_out[...].reshape(out.shape).astype(BF16)
+    writes.append(load(out, out_h, outs.at[2]))
+    writes[2].start()
     for write in writes:
         write.wait()
 
 
-def mlp_grad_kernel(cot_h, grad_h, w_in_h, inv_h, out, inv, cot, grad_b, w_in, sems, *, count):
+def mlp_grad_kernel(cot_h, grad_h, w_in_h, *refs, count, carried):
+    sources, out, targets, refs = refs[:carried], refs[carried], refs[carried + 1 : 2 * carried + 1], refs[2 * carried + 1 :]
+    cot, grad_b, w_in, sems = refs
     chans, hid = w_in.shape
     half = cot.shape[0] // 2
     copies = [load(w_in_h, w_in, sems.at[0])]
@@ -365,7 +378,7 @@
         low, high = pl.ds(n * half, half), pl.ds(n * half // chans * hid, half // chans * hid)
         copies.append(load(cot_h.at[low, :], cot.at[low, :], sems.at[1 + 2 * n]))
         copies.append(load(grad_h.at[high, :], grad_b.at[high, :], sems.at[2 + 2 * n]))
-    copies.append(load(inv_h, inv, sems.at[5]))
+    copies += [load(a, b, sems.at[5 + n]) for n, (a, b) in enumerate(zip(sources, targets))]
     for copy in copies:
         copy.start()
     copies[0].wait()
@@ -378,11 +391,12 @@
         for left in range(0, cot.shape[1], STEP):
             at = slice(left, left + STEP)
             out[low, at] = cot[low, at].astype(F32) + dot(weights, grad_b[high, at])
-    copies[5].wait()
+    for copy in copies[5:]:
+        copy.wait()
 
 
 def back_kernel(
-    blocks, weights, forward, inverse, _, out, modes_h, modes, rows_ref, sems, *, sizes, each,
+    blocks, weights, forward, inverse, _, out_h, modes_h, out, modes, rows_ref, sems, *, sizes, each,
 ):
     layers, cells, owners, owned = sizes
     chans = LANES // (layers * owned)
@@ -427,7 +441,10 @@
         rows_ref[pl.ds(8 + row, owners, 16), :] = jnp.broadcast_to(high, (owners, LANES))
         rows_ref[pl.ds(8 + each + row, owners, 16), :] = jnp.broadcast_to(total - high, (owners, LANES))
     out[...] = rows_ref[...].reshape(out.shape).astype(BF16)
+    send = load(out, out_h, sems.at[1])
+    send.start()
     save.wait()
+    send.wait()
 
 
 def weight_grad_kernel(zx_h, zg_h, out_h, zx, zg, out, sems, *, sizes, factor):
@@ -566,18 +583,19 @@
     grid_mul = 2 * count * n_phi * chans
 
     smalls = (mlp_in, mlp_bias[None], w_out)
-    xp, field_v, w_in_v, bias_v, w_out_v = call(
+    mixing = (spectral_weight, forward, inverse)
+    half = count // 2
+    half_thin = (half * chans, n_phi)
+    xp, field_a, field_b, w_in_v, bias_v, w_out_v = call(
         xp_kernel, "hhhhh",
-        [("v", small, BF16), ("w", thin, BF16), *(("w", x.shape, x.dtype) for x in smalls)],
-        [table, small_rows, ((5,), None)],
+        [("h", small, BF16), *[("w", half_thin, BF16)] * 2, *(("w", x.shape, x.dtype) for x in smalls)],
+        [(small, BF16), table, small_rows, ((7,), None)],
         grid_mul * 2 * n_phi_modes, phi_fwd, field, *smalls, sizes=sizes,
     )
     xp = exchange(xp)
-    half = count // 2
     part = (half * hid, n_phi)
-    half_thin = (half * chans, n_phi)
-
-    def hidden_half(first, after, keep_base, *carried):
+
+    def hidden_half(field, after, keep_base, *carried):
         return call(
             hidden_kernel, "wwwwh" + "h" * len(carried),
             [
@@ -589,41 +607,43 @@
                 ((len(carried),), None), ((3, steps), None),
                 *([(half_thin, F32)] if keep_base == "h" else []),
             ],
-            grid_mul * hid, field_v, w_in_v, bias_v, w_out_v, after, *carried,
-            first=first, count=half, carried=len(carried),
+            grid_mul * hid, field, w_in_v, bias_v, w_out_v, after, *carried,
+            count=half, carried=len(carried),
         )
 
     hidden_a, slope_a, base_a, weights, forward, inverse = hidden_half(
-        0, w_out, "w", spectral_weight, forward, inverse
+        field_a, w_out, "w", *mixing
     )
     wx, zx = call(
-        mix_kernel, "vwww", [("v", small, BF16), ("h", modes, F32)],
-        [(modes, F32), small_rows, ((1,), None)],
+        mix_kernel, "vwww", [("h", small, BF16), ("h", modes, F32)],
+        [(small, BF16), (modes, F32), small_rows, ((2,), None)],
         1 << 24, xp, weights, forward, inverse, sizes=sizes,
     )
     wx = exchange(wx)
-    hidden_b, slope_b, base_b, cot_v, inv_v = hidden_half(half, zx, "h", cot, phi_inv)
+    hidden_b, slope_b, base_b, cot_v, inv_v = hidden_half(field_b, zx, "h", cot, phi_inv)
     gp, hidden_gb = call(
-        gpre_kernel, "vwwwwhhhhhhh", [("v", large, BF16), ("h", tall, BF16)],
+        gpre_kernel, "vwwwwhhhhhhh", [("h", large, BF16), ("h", tall, BF16)],
         [
-            (thin, BF16), (tall, BF16), (tall, BF16), (half_thin, F32), table,
+            (large, BF16), (thin, BF16), (tall, BF16), (tall, BF16), (half_thin, F32), table,
             (thin, BF16), (tall, BF16),
             ((count * chans, 2 * n_phi_modes), BF16), ((half * hid, half * chans), BF16),
             (thin, F32), (tall, F32), small_rows, large_rows, ((hid, LANES), F32),
-            ((3, 3), None), ((2,), None),
+            ((3, 3), None), ((3,), None),
         ],
         grid_mul * (4 * n_phi_modes + 4 * hid), wx, cot_v, base_a, inv_v, w_out_v,
         field, hidden_a, hidden_b, slope_a, slope_b, base_b, phi_fwd, sizes=sizes,
     )
     gp = exchange(gp)
-    partial, inverse_phi = call(
-        mlp_grad_kernel, "hhhh", [("w", thin, F32), ("w", phi_inv.shape, BF16)],
-        [(thin, BF16), (tall, BF16), (mlp_in.shape, BF16), ((6,), None)],
-        grid_mul * hid, cot, hidden_gb, mlp_in, phi_inv, count=half,
+    carried = (phi_inv, *mixing)
+    partial, inverse_phi, weights, forward, inverse = call(
+        mlp_grad_kernel, "hhh" + "h" * len(carried),
+        [("w", thin, F32), *(("w", x.shape, x.dtype) for x in carried)],
+        [(thin, BF16), (tall, BF16), (mlp_in.shape, BF16), ((5 + len(carried),), None)],
+        grid_mul * hid, cot, hidden_gb, mlp_in, *carried, count=half, carried=len(carried),
     )
     wb, zg = call(
-        back_kernel, "vwwww", [("w", large, BF16), ("h", modes, F32)],
-        [(modes, F32), large_rows, ((1,), None)],
+        back_kernel, "vwwww", [("h", large, BF16), ("h", modes, F32)],
+        [(large, BF16), (modes, F32), large_rows, ((2,), None)],
         1 << 24, gp, weights, forward, inverse, partial, sizes=sizes, each=each,
     )
     wb = exchange(wb)

time: 64.5 us -> 61.7 us (0.957)
  local copies, waits for them, and re-layouts: 2.84 us -> 0 us
  waiting for transfers between devices: 18.9 us -> 19.9 us
    unnamed x6 -> x0, local copies, waits for them, and re-layouts: 2.84 us -> none
    all_to_all x4, waiting for transfers between devices: 18.9 us -> 19.9 us  [local(): exchange = lambda x: lax.all_to_all(x, 'eta', 0, 0, tiled=True)]
where the time goes in v3:
time: 61.7 us; the launch traced here: 61.3 us
  Pallas kernels  25.6 us (41%)
  waiting for transfers between devices  19.9 us (32%)
  starting transfers between devices  15.1 us (24%)
  between operations  0.73 us (1%)
    pallas_call x9, Pallas kernels, call(): pl.pallas_call(functools.partial(kernel, **static), out_shape=[keep[o[0]]...  25.6 us
    all_to_all x4, waiting for transfers between devices, local(): exchange = lambda x: lax.all_to_all(x, 'eta', 0, 0, tiled=True)  19.9 us
    all_to_all x4, starting transfers between devices, local(): exchange = lambda x: lax.all_to_all(x, 'eta', 0, 0, tiled=True)  15.1 us
  transfers between devices with their start and end apart: 4, of which 4 were waited for; matrix products, arithmetic and copies ran while one was open for 0% of the time, Pallas kernels for 18%

profile of v3, /device:TPU:0, one launch (start us, length us, event | category | flops | bytes accessed | tf_op | source)
XLA Modules:
  0.0 61.3 jit_solution(5837331925465362833)
XLA Ops:
  0.6 2.7 %shard_map.137 = (bf16[32,8,128]{2,1,0:T(8,128)(2,1)}, bf16[128,2048]{1,0:T(8,128)(2,1)S(1)}, bf16[128,2048]{1,0:T(8,128)(2,1)S(1)}, bf16[32,64]{1,0:T(8,128)(2,...) custom-call(bf16[128,2048]{1,0:T(8,128)(2,1)} %constant.8.clone.fwd_h, bf16[256,2048]{1,0:T(8,128)(2,1)} %bitcast.9, ...), custom_call_target="tpu_custom_call" | custom-call | flops 134217728 | bytes 2703872 | tf_op jit(solution)/shard_map/pallas_call | solution.py:530
  3.3 7.3 %all-to-all-start = ((bf16[32,8,128]{2,1,0:T(8,128)(2,1)}), bf16[32,8,128]{2,1,0:T(8,128)(2,1)S(1)}, u32[]{:S(2)}, u32[]{:S(2)}) async-start(bf16[32,8,128]{2,1,0:T(8,128)(2,1)} %get-tuple-element.37), calls=%async_computation | async-start | bytes 131072 | tf_op jit(solution)/shard_map/all_to_all | solution.py:576
  10.6 3.0 %shard_map.138 = (bf16[256,2048]{1,0:T(8,128)(2,1)}, bf16[256,2048]{1,0:T(8,128)(2,1)}, f32[128,2048]{1,0:T(8,128)S(1)}, bf16[2,2,64,1024]{3,2,1,0:T(8,128)(2,1)...) custom-call(bf16[128,2048]{1,0:T(8,128)(2,1)S(1)} %get-tuple-element.38.field, ...), custom_call_target="tpu_custom_call" | custom-call | flops 67108864 | bytes 5189888 | tf_op jit(solution)/shard_map/pallas_call | solution.py:530
  13.7 4.4 %all-to-all-done.blocks = bf16[32,8,128]{2,1,0:T(8,128)(2,1)S(1)} async-done(((bf16[32,8,128]{2,1,0:T(8,128)(2,1)}), bf16[32,8,128]{2,1,0:T(8,128)(2,1)S(1)}, u32[]{:S(2)}, u32[]{:S(2)}) %all-to-all-start) | async-done | bytes 65568 | tf_op jit(solution)/shard_map/all_to_all | solution.py:576
  18.0 1.9 %shard_map.139 = (bf16[32,8,128]{2,1,0:T(8,128)(2,1)}, f32[128,128]{1,0:T(8,128)}) custom-call(bf16[32,8,128]{2,1,0:T(8,128)(2,1)S(1)} %all-to-all-done.blocks, bf16[2,2,64,1024]{3,2,1,0:T(8,128)(2,1)S(1)} %get-tuple-element.42.weights, bf16[128,128]{1,0:T(8,128)(2,1)S(1)} %get-tuple-element.43.forward, bf16[256,384]{1,0:T(8,128)(2,1)S(1)} %get-tuple-element.44.inverse), custom_call_target="tpu_custom_call" | custom-call | flops 16777216 | bytes 950272 | tf_op jit(solution)/shard_map/pallas_call | solution.py:530
  19.9 2.6 %all-to-all-start.1 = ((bf16[32,8,128]{2,1,0:T(8,128)(2,1)}), bf16[32,8,128]{2,1,0:T(8,128)(2,1)S(1)}, u32[]{:S(2)}, u32[]{:S(2)}) async-start(bf16[32,8,128]{2,1,0:T(8,128)(2,1)} %get-tuple-element.45), calls=%async_computation.1 | async-start | bytes 131072 | tf_op jit(solution)/shard_map/all_to_all | solution.py:576
  22.5 3.8 %shard_map.140 = (bf16[256,2048]{1,0:T(8,128)(2,1)}, bf16[256,2048]{1,0:T(8,128)(2,1)}, f32[128,2048]{1,0:T(8,128)}, bf16[256,2048]{1,0:T(8,128)(2,1)S(1)}, bf16[128,2048]{1,0:T(8,128)(2,1)S(1)}) custom-call(bf16[128,2048]{1,0:T(8,128)(2,1)S(1)} %get-tuple-element.46.field, bf16[32,64]{1,0:T(8,128)(2,1)S(1)} %get-tuple-element.39.w_in, ...), custom_call_target="tpu_custom_call" | custom-call | flops 67108864 | bytes 6889728 | tf_op jit(solution)/shard_map/pallas_call | solution.py:530
  26.3 3.6 %all-to-all-done.1.blocks = bf16[32,8,128]{2,1,0:T(8,128)(2,1)S(1)} async-done(((bf16[32,8,128]{2,1,0:T(8,128)(2,1)}), bf16[32,8,128]{2,1,0:T(8,128)(2,1)S(1)}, u32[]{:S(2)}, u32[]{:S(2)}) %all-to-all-start.1) | async-done | bytes 65568 | tf_op jit(solution)/shard_map/all_to_all | solution.py:576
  29.9 6.1 %shard_map.141 = (bf16[32,16,128]{2,1,0:T(8,128)(2,1)}, bf16[512,2048]{1,0:T(8,128)(2,1)}) custom-call(bf16[32,8,128]{2,1,0:T(8,128)(2,1)S(1)} %all-to-all-done.1.blocks, bf16[256,2048]{1,0:T(8,128)(2,1)S(1)} %get-tuple-element.48.cot, f32[128,2048]{1,0:T(8,128)S(1)} %get-tuple-element.49.base_a, bf16[128,2048]{1,0:T(8,128)(2,1)S(1)} %get-tuple-element.50.inv, ...), custom_call_target="tpu_custom_call" | custom-call | flops 536870912 | bytes 11735040 | tf_op jit(solution)/shard_map/pallas_call | solution.py:530
  36.0 2.6 %all-to-all-start.2 = ((bf16[32,16,128]{2,1,0:T(8,128)(2,1)}), bf16[32,16,128]{2,1,0:T(8,128)(2,1)S(1)}, u32[]{:S(2)}, u32[]{:S(2)}) async-start(bf16[32,16,128]{2,1,0:T(8,128)(2,1)} %get-tuple-element.56), calls=%async_computation.2 | async-start | bytes 262144 | tf_op jit(solution)/shard_map/all_to_all | solution.py:576
  38.6 2.3 %shard_map.142 = (f32[256,2048]{1,0:T(8,128)S(1)}, bf16[128,2048]{1,0:T(8,128)(2,1)S(1)}, bf16[2,2,64,1024]{3,2,1,0:T(8,128)(2,1)S(1)}, bf16[128,128]{1,0:T(8,128)(2,1)S(1)}, bf16[256,384]{1,0:T(8,128)(2,1)S(1)}) custom-call(bf16[256,2048]{1,0:T(8,128)(2,1)} %bitcast.8, bf16[512,2048]{1,0:T(8,128)(2,1)} %get-tuple-element.57.grad_h, bf16[32,64]{1,0:T(8,128)(2,1)} %w_in_h.1, ...), custom_call_target="tpu_custom_call" | custom-call | flops 67108864 | bytes 7802880 | tf_op jit(solution)/shard_map/pallas_call | solution.py:530
  40.9 5.9 %all-to-all-done.2.blocks = bf16[32,16,128]{2,1,0:T(8,128)(2,1)S(1)} async-done(((bf16[32,16,128]{2,1,0:T(8,128)(2,1)}), bf16[32,16,128]{2,1,0:T(8,128)(2,1)S(1)}, u32[]{:S(2)}, u32[]{:S(2)}) %all-to-all-start.2) | async-done | bytes 131104 | tf_op jit(solution)/shard_map/all_to_all | solution.py:576
  46.8 1.8 %shard_map.143 = (bf16[32,16,128]{2,1,0:T(8,128)(2,1)}, f32[128,128]{1,0:T(8,128)}) custom-call(bf16[32,16,128]{2,1,0:T(8,128)(2,1)S(1)} %all-to-all-done.2.blocks, bf16[2,2,64,1024]{3,2,1,0:T(8,128)(2,1)S(1)} %get-tuple-element.58.weights, bf16[128,128]{1,0:T(8,128)(2,1)S(1)} %get-tuple-element.59.forward, bf16[256,384]{1,0:T(8,128)(2,1)S(1)} %get-tuple-element.60.inverse, ...), custom_call_target="tpu_custom_call" | custom-call | flops 16777216 | bytes 3178496 | tf_op jit(solution)/shard_map/pallas_call | solution.py:530
  48.7 2.6 %all-to-all-start.3 = ((bf16[32,16,128]{2,1,0:T(8,128)(2,1)}), bf16[32,16,128]{2,1,0:T(8,128)(2,1)S(1)}, u32[]{:S(2)}, u32[]{:S(2)}) async-start(bf16[32,16,128]{2,1,0:T(8,128)(2,1)} %get-tuple-element.62), calls=%async_computation.3 | async-start | bytes 262144 | tf_op jit(solution)/shard_map/all_to_all | solution.py:576
  51.3 2.2 %shard_map.144._ = f32[2,2,64,1024]{3,2,1,0:T(8,128)} custom-call(f32[128,128]{1,0:T(8,128)} %get-tuple-element.47._.zx_h, f32[128,128]{1,0:T(8,128)} %get-tuple-element.64.zg_h), custom_call_target="tpu_custom_call" | custom-call | flops 16777216 | bytes 1179648 | tf_op jit(solution)/shard_map/pallas_call | solution.py:530
  53.5 6.0 %all-to-all-done.3.blocks = bf16[32,16,128]{2,1,0:T(8,128)(2,1)S(1)} async-done(((bf16[32,16,128]{2,1,0:T(8,128)(2,1)}), bf16[32,16,128]{2,1,0:T(8,128)(2,1)S(1)}, u32[]{:S(2)}, u32[]{:S(2)}) %all-to-all-start.3) | async-done | bytes 131104 | tf_op jit(solution)/shard_map/all_to_all | solution.py:576
  59.5 1.8 %shard_map.145 = (f32[256,2048]{1,0:T(8,128)}, f32[32,64]{1,0:T(8,128)}, f32[32,64]{1,0:T(8,128)}, f32[1,64]{1,0:T(1,128)}) custom-call(bf16[32,16,128]{2,1,0:T(8,128)(2,1)S(1)} %all-to-all-done.3.blocks, f32[256,2048]{1,0:T(8,128)S(1)} %get-tuple-element.61._.base, bf16[128,2048]{1,0:T(8,128)(2,1)S(1)} %get-tuple-element.63.inv, ...), custom_call_target="tpu_custom_call" | custom-call | flops 134217728 | bytes 5914880 | tf_op jit(solution)/shard_map/pallas_call | solution.py:530
Async XLA Ops:
  3.3 14.7 %all-to-all-start = ((bf16[32,8,128]{2,1,0:T(8,128)(2,1)}), bf16[32,8,128]{2,1,0:T(8,128)(2,1)S(1)}, u32[]{:S(2)}, u32[]{:S(2)}) async-start(bf16[32,8,128]{2,1,0:T(8,128)(2,1)} %get-tuple-element.37), calls=%async_computation | async-start | bytes 131072 | tf_op jit(solution)/shard_map/all_to_all | solution.py:576
  19.9 10.0 %all-to-all-start.1 = ((bf16[32,8,128]{2,1,0:T(8,128)(2,1)}), bf16[32,8,128]{2,1,0:T(8,128)(2,1)S(1)}, u32[]{:S(2)}, u32[]{:S(2)}) async-start(bf16[32,8,128]{2,1,0:T(8,128)(2,1)} %get-tuple-element.45), calls=%async_computation.1 | async-start | bytes 131072 | tf_op jit(solution)/shard_map/all_to_all | solution.py:576
  36.0 10.8 %all-to-all-start.2 = ((bf16[32,16,128]{2,1,0:T(8,128)(2,1)}), bf16[32,16,128]{2,1,0:T(8,128)(2,1)S(1)}, u32[]{:S(2)}, u32[]{:S(2)}) async-start(bf16[32,16,128]{2,1,0:T(8,128)(2,1)} %get-tuple-element.56), calls=%async_computation.2 | async-start | bytes 262144 | tf_op jit(solution)/shard_map/all_to_all | solution.py:576
  48.7 10.8 %all-to-all-start.3 = ((bf16[32,16,128]{2,1,0:T(8,128)(2,1)}), bf16[32,16,128]{2,1,0:T(8,128)(2,1)S(1)}, u32[]{:S(2)}, u32[]{:S(2)}) async-start(bf16[32,16,128]{2,1,0:T(8,128)(2,1)} %get-tuple-element.62), calls=%async_computation.3 | async-start | bytes 262144 | tf_op jit(solution)/shard_map/all_to_all | solution.py:576

commit v4 on v3

--- a/solution.py
+++ b/solution.py
@@ -187,7 +187,7 @@
 
 
 def unpack(blocks, rows_ref, cells, owners):
-    rows = blocks.shape[1]
+    rows = rows_ref.shape[0] // owners
     rows_ref[...] = blocks[...].astype(F32).reshape(rows_ref.shape)
     part = lambda p: jnp.concatenate(
         [rows_ref[pl.ds(cell * 2 + p, owners, rows), :] for cell in range(cells)], axis=0
@@ -259,7 +259,7 @@
 
 
 def phi_rows(blocks, rows_ref, layers, cells, owners, owned):
-    rows = blocks.shape[1]
+    rows = rows_ref.shape[0] // owners
     rows_ref[...] = blocks[...].astype(F32).reshape(rows_ref.shape)
     chans = LANES // (layers * owned)
     tall = []
@@ -347,20 +347,18 @@
         copy.wait()
     results.append(products(1))
     spectra = jnp.concatenate([r[0] for r in results], axis=1)
-    pack_spectra(spectra, rows_out, 16, layers, cells, owners, owned)
+    each = hid // owners
+    pack_spectra(spectra, rows_out, 8 + 2 * each, layers, cells, owners, owned)
     part_in, part_out = results[0][1] + results[1][1], results[0][2] + results[1][2]
     bias = jnp.sum(total, axis=1, keepdims=True)
     zeros = jnp.zeros((hid, LANES - 2 * chans), F32)
     full = jnp.concatenate([part_in, part_out, zeros], axis=1)
     full = jnp.where(iota((hid, LANES), 1) == 2 * chans, bias, full)
     high = full.astype(BF16).astype(F32)
-    each = hid // owners
     for at, value in enumerate((high, full - high)):
         slab[...] = value
         for row in range(each):
-            rows_out[pl.ds(8 + at * each + row, owners, 16), :] = slab[pl.ds(row, owners, each), :]
-    for row in range(8 + 2 * each, 16):
-        rows_out[pl.ds(row, owners, 16), :] = jnp.zeros((owners, LANES), F32)
+            rows_out[pl.ds(8 + at * each + row, owners, 8 + 2 * each), :] = slab[pl.ds(row, owners, each), :]
     out[...] = rows_out[...].reshape(out.shape).astype(BF16)
     writes.append(load(out, out_h, outs.at[2]))
     writes[2].start()
@@ -411,7 +409,7 @@
     for row in range(each):
         at = 8 + row
         total = jnp.sum(
-            rows_ref[pl.ds(at, owners, 16), :] + rows_ref[pl.ds(at + each, owners, 16), :],
+            rows_ref[pl.ds(at, owners, 8 + 2 * each), :] + rows_ref[pl.ds(at + each, owners, 8 + 2 * each), :],
             axis=0,
             keepdims=True,
         )
@@ -435,11 +433,11 @@
             acc = s if acc is None else acc + s
         acc = [acc[2 * n * half : 2 * (n + 1) * half] for n in range(layers)]
         pieces += [a[:, :chans] for a in acc]
-    fields_of(jnp.concatenate(pieces, axis=1), inverse, rows_ref, 16, cells, owners)
+    fields_of(jnp.concatenate(pieces, axis=1), inverse, rows_ref, 8 + 2 * each, cells, owners)
     for row, total in enumerate(totals):
         high = total.astype(BF16).astype(F32)
-        rows_ref[pl.ds(8 + row, owners, 16), :] = jnp.broadcast_to(high, (owners, LANES))
-        rows_ref[pl.ds(8 + each + row, owners, 16), :] = jnp.broadcast_to(total - high, (owners, LANES))
+        rows_ref[pl.ds(8 + row, owners, 8 + 2 * each), :] = jnp.broadcast_to(high, (owners, LANES))
+        rows_ref[pl.ds(8 + each + row, owners, 8 + 2 * each), :] = jnp.broadcast_to(total - high, (owners, LANES))
     out[...] = rows_ref[...].reshape(out.shape).astype(BF16)
     send = load(out, out_h, sems.at[1])
     send.start()
@@ -497,7 +495,7 @@
     each = hid // owners
     for row in range(each):
         slab[pl.ds(row, owners, each), :] = (
-            rows_ref[pl.ds(8 + row, owners, 16), :] + rows_ref[pl.ds(8 + each + row, owners, 16), :]
+            rows_ref[pl.ds(8 + row, owners, 8 + 2 * each), :] + rows_ref[pl.ds(8 + each + row, owners, 8 + 2 * each), :]
         ) * norm
     turned[...] = slab[...].T
     writes = [
@@ -574,11 +572,12 @@
     w_out = mlp_out.T
     steps = n_phi // STEP
     exchange = lambda x: lax.all_to_all(x, "eta", 0, 0, tiled=True)
+    exchange_pairs = lambda x: exchange(x.reshape(owners, -1, 2, LANES)).reshape(x.shape)
     small = (owners, 8, LANES)
-    large = (owners, 16, LANES)
+    large = (owners * (8 + 2 * each), LANES)
     modes = (2 * n_eta_modes, LANES)
     small_rows = ((owners * 8, LANES), F32)
-    large_rows = ((owners * 16, LANES), F32)
+    large_rows = (large, F32)
     table = ((2 * n_phi_modes, n_phi), BF16)
     grid_mul = 2 * count * n_phi * chans
 
@@ -633,7 +632,7 @@
         grid_mul * (4 * n_phi_modes + 4 * hid), wx, cot_v, base_a, inv_v, w_out_v,
         field, hidden_a, hidden_b, slope_a, slope_b, base_b, phi_fwd, sizes=sizes,
     )
-    gp = exchange(gp)
+    gp = exchange_pairs(gp)
     carried = (phi_inv, *mixing)
     partial, inverse_phi, weights, forward, inverse = call(
         mlp_grad_kernel, "hhh" + "h" * len(carried),
@@ -646,7 +645,7 @@
         [(large, BF16), (modes, F32), large_rows, ((2,), None)],
         1 << 24, gp, weights, forward, inverse, partial, sizes=sizes, each=each,
     )
-    wb = exchange(wb)
+    wb = exchange_pairs(wb)
     factor = math.sqrt(n_phi * n_eta / (n_phi_modes * n_eta_modes))
     grad_shape = (2, owned, n_eta_modes, chans * chans)
     (grad_spectral,) = call(

time: 61.7 us -> 60.8 us (0.985)
  waiting for transfers between devices: 19.9 us -> 19.1 us
    all_to_all x4, waiting for transfers between devices: 19.9 us -> 19.1 us  [local(): exchange = lambda x: lax.all_to_all(x, 'eta', 0, 0, tiled=True)]
  transfers between devices with their start and end apart: 4 -> 4, of which waited for: 4 -> 4; matrix products, arithmetic and copies ran while one was open for 0% -> 0% of each run, Pallas kernels for 18% -> 19%
where the time goes in v4:
time: 60.8 us; the launch traced here: 60.3 us
  Pallas kernels  25.5 us (42%)
  waiting for transfers between devices  19.1 us (31%)
  starting transfers between devices  15.1 us (25%)
  between operations  0.73 us (1%)
    pallas_call x9, Pallas kernels, call(): pl.pallas_call(functools.partial(kernel, **static), out_shape=[keep[o[0]]...  25.5 us
    all_to_all x4, waiting for transfers between devices, local(): exchange = lambda x: lax.all_to_all(x, 'eta', 0, 0, tiled=True)  19.1 us
    all_to_all x4, starting transfers between devices, local(): exchange = lambda x: lax.all_to_all(x, 'eta', 0, 0, tiled=True)  15.1 us
  transfers between devices with their start and end apart: 4, of which 4 were waited for; matrix products, arithmetic and copies ran while one was open for 0% of the time, Pallas kernels for 19%

profile of v4, /device:TPU:0, one launch (start us, length us, event | category | flops | bytes accessed | tf_op | source)
XLA Modules:
  0.0 60.3 jit_solution(5883169618781683401)
XLA Ops:
  0.6 2.7 %shard_map.137 = (bf16[32,8,128]{2,1,0:T(8,128)(2,1)}, bf16[128,2048]{1,0:T(8,128)(2,1)S(1)}, bf16[128,2048]{1,0:T(8,128)(2,1)S(1)}, bf16[32,64]{1,0:T(8,128)(2,...) custom-call(bf16[128,2048]{1,0:T(8,128)(2,1)} %constant.8.clone.fwd_h, bf16[256,2048]{1,0:T(8,128)(2,1)} %bitcast.15, ...), custom_call_target="tpu_custom_call" | custom-call | flops 134217728 | bytes 2703872 | tf_op jit(solution)/shard_map/pallas_call | solution.py:528
  3.3 7.3 %all-to-all-start = ((bf16[32,8,128]{2,1,0:T(8,128)(2,1)}), bf16[32,8,128]{2,1,0:T(8,128)(2,1)S(1)}, u32[]{:S(2)}, u32[]{:S(2)}) async-start(bf16[32,8,128]{2,1,0:T(8,128)(2,1)} %get-tuple-element.37), calls=%async_computation | async-start | bytes 131072 | tf_op jit(solution)/shard_map/all_to_all | solution.py:574
  10.6 3.0 %shard_map.138 = (bf16[256,2048]{1,0:T(8,128)(2,1)}, bf16[256,2048]{1,0:T(8,128)(2,1)}, f32[128,2048]{1,0:T(8,128)S(1)}, bf16[2,2,64,1024]{3,2,1,0:T(8,128)(2,1)...) custom-call(bf16[128,2048]{1,0:T(8,128)(2,1)S(1)} %get-tuple-element.38.field, ...), custom_call_target="tpu_custom_call" | custom-call | flops 67108864 | bytes 5189888 | tf_op jit(solution)/shard_map/pallas_call | solution.py:528
  13.7 4.4 %all-to-all-done.blocks = bf16[32,8,128]{2,1,0:T(8,128)(2,1)S(1)} async-done(((bf16[32,8,128]{2,1,0:T(8,128)(2,1)}), bf16[32,8,128]{2,1,0:T(8,128)(2,1)S(1)}, u32[]{:S(2)}, u32[]{:S(2)}) %all-to-all-start) | async-done | bytes 65568 | tf_op jit(solution)/shard_map/all_to_all | solution.py:574
  18.0 1.9 %shard_map.139 = (bf16[32,8,128]{2,1,0:T(8,128)(2,1)}, f32[128,128]{1,0:T(8,128)}) custom-call(bf16[32,8,128]{2,1,0:T(8,128)(2,1)S(1)} %all-to-all-done.blocks, bf16[2,2,64,1024]{3,2,1,0:T(8,128)(2,1)S(1)} %get-tuple-element.42.weights, bf16[128,128]{1,0:T(8,128)(2,1)S(1)} %get-tuple-element.43.forward, bf16[256,384]{1,0:T(8,128)(2,1)S(1)} %get-tuple-element.44.inverse), custom_call_target="tpu_custom_call" | custom-call | flops 16777216 | bytes 950272 | tf_op jit(solution)/shard_map/pallas_call | solution.py:528
  19.9 2.6 %all-to-all-start.1 = ((bf16[32,8,128]{2,1,0:T(8,128)(2,1)}), bf16[32,8,128]{2,1,0:T(8,128)(2,1)S(1)}, u32[]{:S(2)}, u32[]{:S(2)}) async-start(bf16[32,8,128]{2,1,0:T(8,128)(2,1)} %get-tuple-element.45), calls=%async_computation.1 | async-start | bytes 131072 | tf_op jit(solution)/shard_map/all_to_all | solution.py:574
  22.5 3.8 %shard_map.140 = (bf16[256,2048]{1,0:T(8,128)(2,1)}, bf16[256,2048]{1,0:T(8,128)(2,1)}, f32[128,2048]{1,0:T(8,128)}, bf16[256,2048]{1,0:T(8,128)(2,1)S(1)}, bf16[128,2048]{1,0:T(8,128)(2,1)S(1)}) custom-call(bf16[128,2048]{1,0:T(8,128)(2,1)S(1)} %get-tuple-element.46.field, bf16[32,64]{1,0:T(8,128)(2,1)S(1)} %get-tuple-element.39.w_in, ...), custom_call_target="tpu_custom_call" | custom-call | flops 67108864 | bytes 6889728 | tf_op jit(solution)/shard_map/pallas_call | solution.py:528
  26.3 3.6 %all-to-all-done.1.blocks = bf16[32,8,128]{2,1,0:T(8,128)(2,1)S(1)} async-done(((bf16[32,8,128]{2,1,0:T(8,128)(2,1)}), bf16[32,8,128]{2,1,0:T(8,128)(2,1)S(1)}, u32[]{:S(2)}, u32[]{:S(2)}) %all-to-all-start.1) | async-done | bytes 65568 | tf_op jit(solution)/shard_map/all_to_all | solution.py:574
  29.9 6.0 %shard_map.141 = (bf16[384,128]{1,0:T(8,128)(2,1)}, bf16[512,2048]{1,0:T(8,128)(2,1)}) custom-call(bf16[32,8,128]{2,1,0:T(8,128)(2,1)S(1)} %all-to-all-done.1.blocks, bf16[256,2048]{1,0:T(8,128)(2,1)S(1)} %get-tuple-element.48.cot, f32[128,2048]{1,0:T(8,128)S(1)} %get-tuple-element.49.base_a, bf16[128,2048]{1,0:T(8,128)(2,1)S(1)} %get-tuple-element.50.inv, ...), custom_call_target="tpu_custom_call" | custom-call | flops 536870912 | bytes 11702272 | tf_op jit(solution)/shard_map/pallas_call | solution.py:528
  36.0 2.6 %all-to-all-start.2 = ((bf16[32,6,2,128]{3,2,1,0:T(2,128)(2,1)}), bf16[32,6,2,128]{3,2,1,0:T(2,128)(2,1)S(1)}, u32[]{:S(2)}, u32[]{:S(2)}) async-start(bf16[32,6,2,128]{3,2,1,0:T(2,128)(2,1)} %bitcast.17), calls=%async_computation.2 | async-start | bytes 196608 | tf_op jit(solution)/shard_map/all_to_all | solution.py:574
  38.6 2.3 %shard_map.142 = (f32[256,2048]{1,0:T(8,128)S(1)}, bf16[128,2048]{1,0:T(8,128)(2,1)S(1)}, bf16[2,2,64,1024]{3,2,1,0:T(8,128)(2,1)S(1)}, bf16[128,128]{1,0:T(8,128)(2,1)S(1)}, bf16[256,384]{1,0:T(8,128)(2,1)S(1)}) custom-call(bf16[256,2048]{1,0:T(8,128)(2,1)} %bitcast.14, bf16[512,2048]{1,0:T(8,128)(2,1)} %get-tuple-element.57.grad_h, bf16[32,64]{1,0:T(8,128)(2,1)} %w_in_h.1, ...), custom_call_target="tpu_custom_call" | custom-call | flops 67108864 | bytes 7802880 | tf_op jit(solution)/shard_map/pallas_call | solution.py:528
  40.9 5.5 %all-to-all-done.2 = bf16[32,6,2,128]{3,2,1,0:T(2,128)(2,1)S(1)} async-done(((bf16[32,6,2,128]{3,2,1,0:T(2,128)(2,1)}), bf16[32,6,2,128]{3,2,1,0:T(2,128)(2,1)S(1)}, u32[]{:S(2)}, u32[]{:S(2)}) %all-to-all-start.2) | async-done | bytes 98336 | tf_op jit(solution)/shard_map/all_to_all | solution.py:574
  46.4 1.8 %shard_map.143 = (bf16[384,128]{1,0:T(8,128)(2,1)}, f32[128,128]{1,0:T(8,128)}) custom-call(bf16[384,128]{1,0:T(8,128)(2,1)S(1)} %bitcast.11, bf16[2,2,64,1024]{3,2,1,0:T(8,128)(2,1)S(1)} %get-tuple-element.58.weights, bf16[128,128]{1,0:T(8,128)(2,1)S(1)} %get-tuple-element.59.forward, bf16[256,384]{1,0:T(8,128)(2,1)S(1)} %get-tuple-element.60.inverse, ...), custom_call_target="tpu_custom_call" | custom-call | flops 16777216 | bytes 3112960 | tf_op jit(solution)/shard_map/pallas_call | solution.py:528
  48.1 2.6 %all-to-all-start.3 = ((bf16[32,6,2,128]{3,2,1,0:T(2,128)(2,1)}), bf16[32,6,2,128]{3,2,1,0:T(2,128)(2,1)S(1)}, u32[]{:S(2)}, u32[]{:S(2)}) async-start(bf16[32,6,2,128]{3,2,1,0:T(2,128)(2,1)} %bitcast.18), calls=%async_computation.3 | async-start | bytes 196608 | tf_op jit(solution)/shard_map/all_to_all | solution.py:574
  50.7 2.2 %shard_map.144._ = f32[2,2,64,1024]{3,2,1,0:T(8,128)} custom-call(f32[128,128]{1,0:T(8,128)} %get-tuple-element.47._.zx_h, f32[128,128]{1,0:T(8,128)} %get-tuple-element.64.zg_h), custom_call_target="tpu_custom_call" | custom-call | flops 16777216 | bytes 1179648 | tf_op jit(solution)/shard_map/pallas_call | solution.py:528
  53.0 5.6 %all-to-all-done.3 = bf16[32,6,2,128]{3,2,1,0:T(2,128)(2,1)S(1)} async-done(((bf16[32,6,2,128]{3,2,1,0:T(2,128)(2,1)}), bf16[32,6,2,128]{3,2,1,0:T(2,128)(2,1)S(1)}, u32[]{:S(2)}, u32[]{:S(2)}) %all-to-all-start.3) | async-done | bytes 98336 | tf_op jit(solution)/shard_map/all_to_all | solution.py:574
  58.6 1.8 %shard_map.145 = (f32[256,2048]{1,0:T(8,128)}, f32[32,64]{1,0:T(8,128)}, f32[32,64]{1,0:T(8,128)}, f32[1,64]{1,0:T(1,128)}) custom-call(bf16[384,128]{1,0:T(8,128)(2,1)S(1)} %bitcast.12, f32[256,2048]{1,0:T(8,128)S(1)} %get-tuple-element.61._.base, bf16[128,2048]{1,0:T(8,128)(2,1)S(1)} %get-tuple-element.63.inv, f32[2,2,64,1024]{3,2,1,0:T(8,128)} %shard_map.144._), custom_call_target="tpu_custom_call" | custom-call | flops 134217728 | bytes 5882112 | tf_op jit(solution)/shard_map/pallas_call | solution.py:528
Async XLA Ops:
  3.3 14.7 %all-to-all-start = ((bf16[32,8,128]{2,1,0:T(8,128)(2,1)}), bf16[32,8,128]{2,1,0:T(8,128)(2,1)S(1)}, u32[]{:S(2)}, u32[]{:S(2)}) async-start(bf16[32,8,128]{2,1,0:T(8,128)(2,1)} %get-tuple-element.37), calls=%async_computation | async-start | bytes 131072 | tf_op jit(solution)/shard_map/all_to_all | solution.py:574
  19.9 10.0 %all-to-all-start.1 = ((bf16[32,8,128]{2,1,0:T(8,128)(2,1)}), bf16[32,8,128]{2,1,0:T(8,128)(2,1)S(1)}, u32[]{:S(2)}, u32[]{:S(2)}) async-start(bf16[32,8,128]{2,1,0:T(8,128)(2,1)} %get-tuple-element.45), calls=%async_computation.1 | async-start | bytes 131072 | tf_op jit(solution)/shard_map/all_to_all | solution.py:574
  36.0 10.4 %all-to-all-start.2 = ((bf16[32,6,2,128]{3,2,1,0:T(2,128)(2,1)}), bf16[32,6,2,128]{3,2,1,0:T(2,128)(2,1)S(1)}, u32[]{:S(2)}, u32[]{:S(2)}) async-start(bf16[32,6,2,128]{3,2,1,0:T(2,128)(2,1)} %bitcast.17), calls=%async_computation.2 | async-start | bytes 196608 | tf_op jit(solution)/shard_map/all_to_all | solution.py:574
  48.1 10.4 %all-to-all-start.3 = ((bf16[32,6,2,128]{3,2,1,0:T(2,128)(2,1)}), bf16[32,6,2,128]{3,2,1,0:T(2,128)(2,1)S(1)}, u32[]{:S(2)}, u32[]{:S(2)}) async-start(bf16[32,6,2,128]{3,2,1,0:T(2,128)(2,1)} %bitcast.18), calls=%async_computation.3 | async-start | bytes 196608 | tf_op jit(solution)/shard_map/all_to_all | solution.py:574
